TPU v7x, 32 devices: a whole 2x2x4 slice. The times are simulated.
32 devices in a mesh: groups: 2 (over x), slab: 16 (over z, y, core).
Axes of the slice: x: 2, y: 2, z: 4, core: 2. Of those that a mesh axis runs over, the one named last changes fastest.
Arguments:
- latent: bfloat16 [64, 32, 2048], P(None, ('groups', 'slab')), parts along dimension 1, may hold values from -6 to 6
- conv1_weight: bfloat16 [27, 64, 64], replicated, may hold values from -0.15625 to 0.15625
- conv2_weight: bfloat16 [27, 64, 64], replicated, may hold values from -0.15625 to 0.15625
- head: bfloat16 [64], replicated, may hold values from -2 to 2
- p_prev: float32 [32, 16, 64, 128], P(('groups', 'slab')), parts along dimension 0, may hold values from -6 to 6
- p_cur: float32 [32, 16, 64, 128], P(('groups', 'slab')), parts along dimension 0, may hold values from -6 to 6
- adjoint: bfloat16 [4, 32, 16, 64, 128], P(None, ('groups', 'slab')), parts along dimension 1, may hold values from -6 to 6
- wavelet: float32 [16, 4], P('groups'), parts along dimension 0, may hold values from -12 to 12
- sources: int32 [16, 3], P('groups'), parts along dimension 0, may hold values from 0 to 127, as said below
- receivers: int32 [16, 3, 128], P('groups'), parts along dimension 0, may hold values from 0 to 127, as said below
Outputs:
- pressure_final: float32 [32, 16, 64, 128], P(('groups', 'slab')), parts along dimension 0
- traces: float32 [16, 4, 128], P('groups'), parts along dimension 0
- gradient: float32 [32, 2048], P(('groups', 'slab')), parts along dimension 0
There are 2 independent parts, one for each index of `groups`. A program takes and returns all parts, laid end to end along the dimension named above; an argument that names none is the same for every part. Nothing has to cross between parts.
Inputs may be any that keep to these rules, and one draw needn't show every extreme that they name: sources[s] is the source cell (depth, row, column) of shot s on the fine grid: depth below 32, row below 64, column below 128. receivers[s, :, k] is the cell (depth, row, column) of receiver k of shot s on the fine grid: depth below 32, row below 64, column below 128.
All inputs are finite; a program needn't handle non-finite values.
Results may differ from a plain program's by a relative error of at most 0.006.
Values may be sent and summed in bfloat16 or wider, within the bound.
A program may use at most 64 MiB of HBM per device.

v0:
```python
import functools

import jax
import jax.numpy as jnp
import numpy as np
from jax import lax
from jax.experimental import pallas as pl
from jax.experimental.pallas import tpu as pltpu
from jax.sharding import PartitionSpec as P

CY = 32
CX = 64
CELLS = CY * CX
CH = 64
SHOTS = 8
STEPS = 4
FPS = 16
FY = 64
FX = 128
VMEM_BYTES = 60 * 2**20
PARTS = 4

C = (-205.0 / 72.0, 8.0 / 5.0, -1.0 / 5.0, 8.0 / 315.0, -1.0 / 560.0)
COURANT = 0.088
LEAK = 0.2
F32 = jnp.float32
BF16 = jnp.bfloat16


def banded(n):
    t = np.zeros((n, n), np.float64)
    for k in range(5):
        for i in range(n):
            for j in {i - k, i + k}:
                if 0 <= j < n:
                    t[i, j] = C[k]
    hi = t.astype(jnp.bfloat16).astype(np.float64)
    return hi, t - hi


def doubling(n):
    u = np.zeros((2 * n, n))
    for k in range(n):
        u[2 * k, k] += 0.75
        u[2 * k, max(k - 1, 0)] += 0.25
        u[2 * k + 1, k] += 0.75
        u[2 * k + 1, min(k + 1, n - 1)] += 0.25
    return u


def constants():
    hi, lo = banded(FX)
    along_x = np.concatenate([hi, hi, lo], axis=0)
    hi, lo = banded(FY)
    four = np.eye(4)
    along_y = np.concatenate([np.kron(four, hi), np.kron(four, hi), np.kron(four, lo)], axis=1)
    depth = np.zeros((FPS, SHOTS + 2))
    for k in range(SHOTS):
        depth[2 * k, k + 1] = 0.75
        depth[2 * k, k] = 0.25
        depth[2 * k + 1, k + 1] = 0.75
        depth[2 * k + 1, k + 2] = 0.25
    rows = doubling(CY)
    up_zy = np.concatenate([np.kron(depth, rows[:, 0::2]), np.kron(depth, rows[:, 1::2])], axis=1)
    up_x = np.kron(np.eye(2), doubling(CX).T)
    out = (along_x, along_y, up_zy, up_zy.T, up_x, up_x.T)
    return [jnp.asarray(a.astype(jnp.bfloat16)) for a in out]


def dot(a, b, dims=((1,), (0,))):
    return lax.dot_general(a, b, (dims, ((), ())), preferred_element_type=F32)


def two(v):
    hi = v.astype(BF16)
    return hi, (v - hi.astype(F32)).astype(BF16)


def kernel(
    n,
    latent,
    w1_hbm,
    w2_hbm,
    head_hbm,
    wavelet_hbm,
    sources_hbm,
    receivers_hbm,
    along_x_hbm,
    along_y_hbm,
    up_x_hbm,
    up_xt_hbm,
    prev_hbm,
    cur_hbm,
    adj_hbm,
    up_zy_hbm,
    up_zyt_hbm,
    final_out,
    traces_out,
    gradient_out,
    head,
    w1,
    w2,
    wavelet,
    sources,
    receivers,
    along_x,
    along_y,
    up_x,
    up_xt,
    lap0,
    head_col,
    a1,
    a2,
    wp1,
    wp2,
    y,
    vel,
    vels,
    field,
    adj,
    up_zy,
    up_zyt,
    speed,
    corr,
    rim_out,
    rim_in,
    hot,
    rec,
    recs,
    gr,
    grs,
    total,
    local_sem,
    lat_s,
    lat_r,
    hid_s,
    hid_r,
    rim_s,
    rim_r,
    vel_s,
    vel_r,
    rec_s,
    rec_r,
    gr_s,
    gr_r,
):
    me = lax.axis_index("slab")
    shot = lax.rem(me, SHOTS)
    slab = me // SHOTS
    slabs = n // SHOTS
    has_low = slab > 0
    has_high = slab < slabs - 1

    inner = pl.ds(4, FPS)
    pairs = (
        (latent, a1.at[1]),
        (w1_hbm, w1),
        (cur_hbm, field.at[1, inner]),
        (w2_hbm, w2),
        (receivers_hbm, receivers),
        (along_y_hbm, along_y),
        (along_x_hbm, along_x),
        (adj_hbm, adj),
        (up_x_hbm, up_x),
        (up_zy_hbm, up_zy),
        (wavelet_hbm, wavelet),
        (sources_hbm, sources),
        (prev_hbm, field.at[0, inner]),
        (up_zyt_hbm, up_zyt),
        (up_xt_hbm, up_xt),
        (head_hbm, head),
    )
    loads = [
        pltpu.make_async_copy(src, dst, local_sem.at[i]) for i, (src, dst) in enumerate(pairs)
    ]

    def remote(src, dst, send, recv, target):
        return pltpu.make_async_remote_copy(
            src_ref=src,
            dst_ref=dst,
            send_sem=send,
            recv_sem=recv,
            device_id={"slab": target},
            device_id_type=pl.DeviceIdType.MESH,
        )

    def peer(j):
        return lax.rem(me + j, n)

    barrier = pltpu.get_barrier_semaphore()

    def greet(j, carry):
        pl.semaphore_signal(
            barrier, inc=1, device_id={"slab": peer(j)}, device_id_type=pl.DeviceIdType.MESH
        )
        return carry

    lax.fori_loop(1, n, greet, 0)
    for load in loads:
        load.start()

    for a in (a1, a2):

        @pl.when(me == 0)
        def _():
            a[0] = jnp.zeros((CH, CELLS), BF16)

        @pl.when(me == n - 1)
        def _():
            a[2] = jnp.zeros((CH, CELLS), BF16)

    pl.semaphore_wait(barrier, n - 1)

    width = CELLS // PARTS

    def lat_copy(side, part):
        cols = pl.ds(part * width, width)
        return remote(
            latent.at[:, cols],
            a1.at[2 * side, :, cols],
            lat_s.at[side, part],
            lat_r.at[side, part],
            peer(1 if side == 0 else n - 1),
        )

    height = CH // PARTS

    def hid_copy(side, part):
        rows = pl.ds(pl.multiple_of(part * height, height), height)
        return remote(
            a2.at[1, rows],
            a2.at[2 * side, rows],
            hid_s.at[side, part],
            hid_r.at[side, part],
            peer(1 if side == 0 else n - 1),
        )

    def rim_copy(side, step):
        return remote(
            rim_out.at[side, step],
            rim_in.at[side, step],
            rim_s.at[side, step],
            rim_r.at[side, step],
            peer(SHOTS if side == 0 else n - SHOTS),
        )

    sends = (me < n - 1, me > 0)
    gets = (me > 0, me < n - 1)
    rim_sends = (has_high, has_low)
    rim_gets = (has_low, has_high)

    for part in range(PARTS):
        for side in range(2):

            @pl.when(sends[side])
            def _():
                lat_copy(side, part).start()

    loads[1].wait()
    loads[3].wait()
    for w, packed in ((w1, wp1), (w2, wp2)):
        for tap in range(9):
            for dz in range(3):
                packed[tap * CH : (tap + 1) * CH, dz * CH : (dz + 1) * CH] = w[dz * 9 + tap]

    loads[2].wait()
    rim_out[0, 0] = field[1, FPS : FPS + 4].reshape(4 * FY, FX).astype(BF16)
    rim_out[1, 0] = field[1, 4:8].reshape(4 * FY, FX).astype(BF16)
    @pl.when(jnp.logical_not(has_low))
    def _():
        field[:, 0:4] = jnp.zeros((2, 4, FY, FX), F32)

    @pl.when(jnp.logical_not(has_high))
    def _():
        field[:, FPS + 4 :] = jnp.zeros((2, 4, FY, FX), F32)

    loads[4].wait()
    loads[15].wait()
    station = receivers[:, shot]
    station_row = (station[0:1] - slab * FPS) * FY + station[1:2]
    station_col = station[2:3]
    hot[...] = (
        (lax.broadcasted_iota(jnp.int32, (FPS * FY, FX), 0) == station_row)
        .astype(F32)
        .astype(BF16)
    )
    col_hot = (lax.broadcasted_iota(jnp.int32, (FX, FX), 0) == station_col).astype(F32)
    rec[...] = jnp.zeros((8, FX), F32)

    square = (CH, CH)
    diagonal = lax.broadcasted_iota(jnp.int32, square, 0) == lax.broadcasted_iota(
        jnp.int32, square, 1
    )
    spread = jnp.broadcast_to(head[...].astype(F32), square)
    head_col[...] = jnp.broadcast_to(
        jnp.sum(jnp.where(diagonal, spread, 0.0), axis=1, keepdims=True), (CH, 128)
    )

    cell = lax.broadcasted_iota(jnp.int32, (1, CELLS), 1)
    col = lax.rem(cell, CX)
    keep_left = (col > 0).astype(F32)
    keep_right = (col < CX - 1).astype(F32)
    keep_up = (cell >= CX).astype(F32)
    keep_down = (cell < CELLS - CX).astype(F32)

    def multiply(packed, a, part):
        cols = slice(part * width, (part + 1) * width)
        block = jnp.concatenate([a[0, :, cols], a[1, :, cols], a[2, :, cols]], axis=0)
        y[:, :, cols] = dot(packed[...], block).reshape(9, CH, width)

    def gathered(first):
        sums = []
        for dx in range(3):
            above = y[dx, pl.ds(first, 8)]
            middle = y[3 + dx, pl.ds(first, 8)]
            below = y[6 + dx, pl.ds(first, 8)]
            sums.append(
                middle
                + keep_up * pltpu.roll(above, CX, 1)
                + keep_down * pltpu.roll(below, CELLS - CX, 1)
            )
        v = (
            sums[1]
            + keep_left * pltpu.roll(sums[0], 1, 1)
            + keep_right * pltpu.roll(sums[2], CELLS - 1, 1)
        )
        return jnp.where(v > 0, v, LEAK * v)

    loads[0].wait()
    for part in range(PARTS):
        for side in range(2):

            @pl.when(gets[side])
            def _():
                lat_copy(side, part).wait_recv()

        multiply(wp1, a1, part)

    for side in range(2):

        @pl.when(rim_sends[side])
        def _():
            rim_copy(side, 0).start()

    def hidden_part(part, carry):
        first = pl.multiple_of(part * height, height)
        pieces = [gathered(pl.multiple_of(first + 8 * h, 8)) for h in range(height // 8)]
        a2[1, pl.ds(first, height)] = jnp.concatenate(pieces, axis=0).astype(BF16)
        for side in range(2):

            @pl.when(sends[side])
            def _():
                hid_copy(side, part).start()

        return carry

    lax.fori_loop(0, PARTS, hidden_part, 0)
    def in_plane(cur, chunks):
        centres = [field[cur, 4 + 4 * c : 8 + 4 * c].reshape(4 * FY, FX) for c in chunks]
        halves = [two(v) for v in centres]
        across = jnp.concatenate(
            [jnp.concatenate([hi, lo, hi], axis=0) for hi, lo in halves], axis=1
        )
        from_rows = dot(along_y[...], across)
        laps = []
        for i, c in enumerate(chunks):
            hi, lo = halves[i]
            lap = from_rows[:, FX * i : FX * (i + 1)]
            lap = lap + dot(jnp.concatenate([hi, lo, hi], axis=1), along_x[...])
            laps.append(lap + C[0] * centres[i])
        return laps

    def in_depth(cur, chunks, laps):
        whole = []
        for c, lap in zip(chunks, laps):
            at = 4 + 4 * c
            for k in range(1, 5):
                near = field[cur, at - k : at - k + 4] + field[cur, at + k : at + k + 4]
                lap = lap + C[k] * near.reshape(4 * FY, FX)
            whole.append(lap)
        return whole

    def laplace(cur, chunks):
        return in_depth(cur, chunks, in_plane(cur, chunks))

    def advance(t, cur, old, c, lap):
        at = 4 + 4 * c
        courant = COURANT * speed[4 * FY * c : 4 * FY * (c + 1)]
        pulse = jnp.where(linear == source_at - c * 4 * FY * FX, wavelet[t, shot], 0.0)
        v = field[cur, at : at + 4].reshape(4 * FY, FX)
        before = field[old, at : at + 4].reshape(4 * FY, FX)
        new = 2.0 * v - before + courant * courant * lap + pulse
        field[old, at : at + 4] = new.reshape(4, FY, FX)

    def weighted(t, c, lap):
        return adj[t, 4 * c : 4 * c + 4].reshape(4 * FY, FX).astype(F32) * lap

    def take_rims(t, cur):
        for side in range(2):

            @pl.when(rim_gets[side])
            def _():
                rim_copy(side, t).wait_recv()
                at = (FPS + 4) * side
                field[cur, at : at + 4] = rim_in[side, t].reshape(4, FY, FX).astype(F32)

    def give_rims(t, old):
        rim_out[0, t + 1] = field[old, FPS : FPS + 4].reshape(4 * FY, FX).astype(BF16)
        rim_out[1, t + 1] = field[old, 4:8].reshape(4 * FY, FX).astype(BF16)
        for side in range(2):

            @pl.when(rim_sends[side])
            def _():
                rim_copy(side, t + 1).start()

    def record(t, old):
        hi, lo = two(field[old, 4 : 4 + FPS].reshape(FPS * FY, FX))
        seen = dot(hi, hot[...], ((0,), (0,))) + dot(lo, hot[...], ((0,), (0,)))
        seen = jnp.sum(seen * col_hot, axis=0, keepdims=True)
        rec[...] += jnp.where(lax.broadcasted_iota(jnp.int32, (8, FX), 0) == t, seen, 0.0)

    for i in (5, 6, 7, 8, 9, 10, 11, 12):
        loads[i].wait()
    source_at = (
        (sources[0, shot] - slab * FPS) * (FY * FX) + sources[1, shot] * FX + sources[2, shot]
    )
    linear = lax.broadcasted_iota(jnp.int32, (4 * FY, FX), 0) * FX + lax.broadcasted_iota(
        jnp.int32, (4 * FY, FX), 1
    )

    take_rims(0, 1)
    for chunks in ((0, 3), (1, 2)):
        for c, lap in zip(chunks, laplace(1, chunks)):
            rows = slice(4 * FY * c, 4 * FY * (c + 1))
            lap0[rows] = lap
            corr[rows] = weighted(0, c, lap)
    for part in range(PARTS):
        for side in range(2):

            @pl.when(gets[side])
            def _():
                hid_copy(side, part).wait_recv()

    for part in range(PARTS):
        multiply(wp2, a2, part)

    def logit_part(part, acc):
        first = pl.multiple_of(part * 8, 8)
        return acc + head_col[pl.ds(first, 8), 0:1] * gathered(first)

    logits = jnp.sum(
        lax.fori_loop(0, CH // 8, logit_part, jnp.zeros((8, CELLS), F32)), axis=0, keepdims=True
    )
    wave_speed = 1.5 + 3.0 / (1.0 + jnp.exp(-logits))
    rows16 = jnp.concatenate(
        [wave_speed[:, FX * j : FX * (j + 1)] for j in range(CELLS // FX)], axis=0
    )
    vel[...] = rows16.astype(BF16)

    def vel_copy(j):
        return remote(vel, vels.at[j], vel_s.at[j], vel_r.at[j], peer(j))

    def rec_copy(j):
        return remote(rec, recs.at[j], rec_s.at[j], rec_r.at[j], peer(j))

    def over_peers(what):
        def one(j, carry):
            what(j)
            return carry

        lax.fori_loop(1, n, one, 0)

    over_peers(lambda j: vel_copy(j).start())
    vels[0] = vel[...]
    over_peers(lambda j: vel_copy(j).wait_recv())

    planes = []
    for i in range(SHOTS + 2):
        plane = jnp.clip(slab * SHOTS - 1 + i, 0, n - 1)
        planes.append(vels[lax.rem(me - plane + n, n)])
    wide = dot(jnp.concatenate(planes, axis=0), up_x[...])
    tall = jnp.concatenate([wide[:, :FX], wide[:, FX:]], axis=0)
    hi, lo = two(tall)
    speed[...] = dot(up_zy[...], hi) + dot(up_zy[...], lo)

    def step(t, carry):
        cur = lax.rem(t + 1, 2)
        old = lax.rem(t, 2)
        outer, middle = (0, 3), (1, 2)
        laps = in_plane(cur, outer)
        take_rims(t, cur)
        laps = in_depth(cur, outer, laps)
        for c, lap in zip(outer, laps):
            advance(t, cur, old, c, lap)
        pl.when(t < STEPS - 1)(lambda: give_rims(t, old))
        laps = laps + laplace(cur, middle)
        for c, lap in zip(middle, laps[2:]):
            advance(t, cur, old, c, lap)
        for c, lap in zip(outer + middle, laps):
            corr[4 * FY * c : 4 * FY * (c + 1)] += weighted(t, c, lap)
        record(t, old)
        return carry

    for chunks in ((0, 3), (1, 2)):
        for c in chunks:
            advance(0, 1, 0, c, lap0[4 * FY * c : 4 * FY * (c + 1)])
        if chunks[0] == 0:
            give_rims(0, 0)
    record(0, 0)
    lax.fori_loop(1, STEPS, step, 0)
    store = pltpu.make_async_copy(
        field.at[(STEPS + 1) % 2, inner], final_out, local_sem.at[len(pairs)]
    )
    store.start()
    over_peers(lambda j: rec_copy(j).start())

    fine = (2.0 * COURANT * COURANT) * speed[...] * corr[...]
    hi, lo = two(fine)
    loads[13].wait()
    loads[14].wait()
    tall = dot(up_zyt[...], hi) + dot(up_zyt[...], lo)
    half = tall.shape[0] // 2
    hi, lo = two(jnp.concatenate([tall[:half], tall[half:]], axis=1))
    narrow = dot(hi, up_xt[...]) + dot(lo, up_xt[...])
    gr[...] = narrow.reshape(SHOTS + 2, 16, FX)

    @pl.when(jnp.logical_not(has_low))
    def _():
        gr[1] += gr[0]

    @pl.when(jnp.logical_not(has_high))
    def _():
        gr[SHOTS] += gr[SHOTS + 1]

    def gr_copy(j):
        other = lax.rem(shot + j, SHOTS)
        return remote(
            gr.at[other + 1], grs.at[j], gr_s.at[j], gr_r.at[j], slab * SHOTS + other
        )

    def low_copy(slot):
        return remote(
            gr.at[0], grs.at[slot], gr_s.at[8], gr_r.at[slot], lax.rem(slab * SHOTS - 1 + n, n)
        )

    def high_copy(slot):
        return remote(
            gr.at[SHOTS + 1],
            grs.at[slot],
            gr_s.at[9],
            gr_r.at[slot],
            lax.rem((slab + 1) * SHOTS, n),
        )

    @pl.when(has_low)
    def _():
        low_copy(8 + shot).start()

    @pl.when(has_high)
    def _():
        high_copy(16 + shot).start()

    for j in range(1, SHOTS):
        gr_copy(j).start()


    recs[0] = rec[...]
    over_peers(lambda j: rec_copy(j).wait_recv())
    for s in range(SHOTS):

        def slab_term(k, acc):
            return acc + recs[lax.rem(me - (k * SHOTS + s) + n, n)]

        summed = lax.fori_loop(0, slabs, slab_term, jnp.zeros((8, FX), F32))
        traces_out[s] = summed[:STEPS]

    total[...] = gr[shot + 1]
    for j in range(1, SHOTS):
        gr_copy(j).wait_recv()
        total[...] += grs[j]

    @pl.when((shot == SHOTS - 1) & has_high)
    def _():
        for s in range(SHOTS):
            low_copy(8 + s).wait_recv()
            total[...] += grs[8 + s]

    @pl.when((shot == 0) & has_low)
    def _():
        for s in range(SHOTS):
            high_copy(16 + s).wait_recv()
            total[...] += grs[16 + s]

    gradient_out[...] = total[...]

    store.wait()
    for part in range(PARTS):
        for side in range(2):

            @pl.when(sends[side])
            def _():
                lat_copy(side, part).wait_send()
                hid_copy(side, part).wait_send()

    for t in range(STEPS):
        for side in range(2):

            @pl.when(rim_sends[side])
            def _():
                rim_copy(side, t).wait_send()

    over_peers(lambda j: vel_copy(j).wait_send())
    over_peers(lambda j: rec_copy(j).wait_send())
    for j in range(1, SHOTS):
        gr_copy(j).wait_send()

    @pl.when(has_low)
    def _():
        low_copy(8 + shot).wait_send()

    @pl.when(has_high)
    def _():
        high_copy(16 + shot).wait_send()


def hand_over(a, b, c, x, y, z, sem):
    copies = [
        pltpu.make_async_copy(src, dst, sem.at[i])
        for i, (src, dst) in enumerate(((a, x), (b, y), (c, z)))
    ]
    for copy in copies:
        copy.start()
    for copy in copies:
        copy.wait()


def body(
    n,
    latent,
    conv1_weight,
    conv2_weight,
    head,
    p_prev,
    p_cur,
    adjoint,
    wavelet,
    sources,
    receivers,
):
    along_x, along_y, up_zy, up_zyt, up_x, up_xt = constants()
    vmem = pl.BlockSpec(memory_space=pltpu.VMEM)
    hbm = pl.BlockSpec(memory_space=pl.ANY)
    dma = pltpu.SemaphoreType.DMA
    final, traces, gradient = pl.pallas_call(
        functools.partial(kernel, n),
        out_shape=(
            pltpu.VMEM((FPS, FY, FX), F32),
            pltpu.VMEM((SHOTS, STEPS, 128), F32),
            pltpu.VMEM((16, FX), F32),
        ),
        in_specs=[hbm] * 16,
        out_specs=(vmem, vmem, vmem),
        scratch_shapes=[
            pltpu.VMEM((1, CH), BF16),
            pltpu.VMEM(conv1_weight.shape, BF16),
            pltpu.VMEM(conv2_weight.shape, BF16),
            pltpu.SMEM((STEPS, SHOTS), F32),
            pltpu.SMEM((3, SHOTS), jnp.int32),
            pltpu.VMEM((3, SHOTS, 128), jnp.int32),
            pltpu.VMEM(along_x.shape, BF16),
            pltpu.VMEM(along_y.shape, BF16),
            pltpu.VMEM(up_x.shape, BF16),
            pltpu.VMEM(up_xt.shape, BF16),
            pltpu.VMEM((FPS * FY, FX), F32),
            pltpu.VMEM((CH, 128), F32),
            pltpu.VMEM((3, CH, CELLS), BF16),
            pltpu.VMEM((3, CH, CELLS), BF16),
            pltpu.VMEM((9 * CH, 3 * CH), BF16),
            pltpu.VMEM((9 * CH, 3 * CH), BF16),
            pltpu.VMEM((9, CH, CELLS), F32),
            pltpu.VMEM((16, FX), BF16),
            pltpu.VMEM((n, 16, FX), BF16),
            pltpu.VMEM((2, FPS + 8, FY, FX), F32),
            pltpu.VMEM((STEPS, FPS, FY, FX), BF16),
            pltpu.VMEM(up_zy.shape, BF16),
            pltpu.VMEM(up_zyt.shape, BF16),
            pltpu.VMEM((FPS * FY, FX), F32),
            pltpu.VMEM((FPS * FY, FX), F32),
            pltpu.VMEM((2, STEPS, 4 * FY, FX), BF16),
            pltpu.VMEM((2, STEPS, 4 * FY, FX), BF16),
            pltpu.VMEM((FPS * FY, FX), BF16),
            pltpu.VMEM((8, FX), F32),
            pltpu.VMEM((n, 8, FX), F32),
            pltpu.VMEM((SHOTS + 2, 16, FX), F32),
            pltpu.VMEM((3 * SHOTS, 16, FX), F32),
            pltpu.VMEM((16, FX), F32),
            dma((17,)),
            dma((2, PARTS)),
            dma((2, PARTS)),
            dma((2, PARTS)),
            dma((2, PARTS)),
            dma((2, STEPS)),
            dma((2, STEPS)),
            dma((n,)),
            dma((n,)),
            dma((n,)),
            dma((n,)),
            dma((10,)),
            dma((3 * SHOTS,)),
        ],
        compiler_params=pltpu.CompilerParams(
            collective_id=0, has_side_effects=True, vmem_limit_bytes=VMEM_BYTES
        ),
    )(
        latent.reshape(CH, CELLS),
        conv1_weight,
        conv2_weight,
        head.reshape(1, CH),
        wavelet.T,
        sources.T,
        receivers.transpose(1, 0, 2),
        along_x,
        along_y,
        up_x,
        up_xt,
        p_prev[0],
        p_cur[0],
        adjoint[:, 0],
        up_zy,
        up_zyt,
    )
    final, traces, gradient = pl.pallas_call(
        hand_over,
        out_shape=(
            jax.ShapeDtypeStruct((FPS, FY, FX), F32),
            jax.ShapeDtypeStruct((SHOTS, STEPS, 128), F32),
            jax.ShapeDtypeStruct((16, FX), F32),
        ),
        in_specs=[vmem] * 3,
        out_specs=[hbm] * 3,
        scratch_shapes=[dma((3,))],
    )(*[pltpu.with_memory_space_constraint(v, pltpu.VMEM) for v in (final, traces, gradient)])
    return final[None], traces, gradient.reshape(1, CELLS)


def solution(mesh):
    in_specs = (
        P(None, ("groups", "slab"), None),
        P(),
        P(),
        P(),
        P(("groups", "slab"), None, None, None),
        P(("groups", "slab"), None, None, None),
        P(None, ("groups", "slab"), None, None, None),
        P("groups", None),
        P("groups", None),
        P("groups", None, None),
    )
    out_specs = (
        P(("groups", "slab"), None, None, None),
        P("groups", None, None),
        P(("groups", "slab"), None),
    )
    return jax.shard_map(
        functools.partial(body, mesh.shape["slab"]),
        mesh=mesh,
        in_specs=in_specs,
        out_specs=out_specs,
        check_vma=False,
    )
```

profile of v0, /device:TPU:0, one launch (start us, length us, event | category | flops | bytes accessed | tf_op | source)
XLA Modules:
  0.0 49.9 jit_solution(10963113082217922948)
XLA Ops:
  0.6 48.5 %shard_map.175 = (f32[16,64,128]{2,1,0:T(8,128)S(1)}, f32[8,4,128]{2,1,0:T(4,128)S(1)}, f32[16,128]{1,0:T(8,128)S(1)}) custom-call(bf16[64,2048]{1,0:T(8,128)(2,1)} %bitcast.13, bf16[27,64,64]{2,1,0:T(8,128)(2,1)} %w1_hbm.1, bf16[27,64,64]{2,1,0:T(8,128)(2,1)} %w2_hbm.1, bf16[1,64]{1,0:T(2,128)(2,1)} %bitcast.17, f32[4,8]{1,0:T(4,128)} %bitcast.15, ...), custom_call_target="tpu_custom_call" | custom-call | tf_op jit(solution)/shard_map/pallas_call | solution.py:654
  49.1 0.8 %shard_map.176 = (f32[16,64,128]{2,1,0:T(8,128)}, f32[8,4,128]{2,1,0:T(4,128)}, f32[16,128]{1,0:T(8,128)}) custom-call(f32[16,64,128]{2,1,0:T(8,128)S(1)} %get-tuple-element.9.a, f32[8,4,128]{2,1,0:T(4,128)S(1)} %get-tuple-element.10.b, f32[16,128]{1,0:T(8,128)S(1)} %get-tuple-element.11.c), custom_call_target="tpu_custom_call" | custom-call | tf_op jit(solution)/shard_map/pallas_call | solution.py:732
where the time goes:
time: 50.1 us; the launch traced here: 49.9 us
  Pallas kernels  49.3 us (98%)
  between operations  0.64 us (1%)
    pallas_call x1, Pallas kernels, body(): pl.pallas_call(functools.partial(kernel, n), out_shape=(pltpu.VMEM((FPS,...  48.5 us

commit v1 on v0

v1 whole, which is shorter than its diff:
```python
import functools

import jax
import jax.numpy as jnp
import numpy as np
from jax import lax
from jax.experimental import pallas as pl
from jax.experimental.pallas import tpu as pltpu
from jax.sharding import PartitionSpec as P

CY = 32
CX = 64
CELLS = CY * CX
CH = 64
SHOTS = 8
STEPS = 4
FPS = 16
FY = 64
FX = 128
VMEM_BYTES = 60 * 2**20
PAIRS = ((0, 3), (3, 5), (5, 7), (7, 8))
FIRST = ((1, 2, 3, 4), (5, 6, 7, 8), (9, 10, 11, 12), (13, 14, 15, 0))
PIECES = ((1, 5), (5, 9), (9, 13), (13, 16), (0, 1))
SECOND = ((2, 3), (4, 5, 6, 7), (8, 9, 10, 11), (12, 13, 14, 15, 0, 1))
COLS = CY // 2

C = (-205.0 / 72.0, 8.0 / 5.0, -1.0 / 5.0, 8.0 / 315.0, -1.0 / 560.0)
BLOCK = 4 * FY
WINDOW = 8 * BLOCK
GROUP = 7
SCALE = 5040.0
CENTRE = 3.0 * SCALE * C[0]
COURANT = 0.088
LEAK = 0.2
F32 = jnp.float32
BF16 = jnp.bfloat16


def near(i, j):
    k = abs(i - j)
    return SCALE * C[k] if 1 <= k <= 4 else 0.0


def banded(n):
    return np.array([[near(i, j) for j in range(n)] for i in range(n)])


def doubling(n):
    u = np.zeros((2 * n, n))
    for k in range(n):
        u[2 * k, k] += 0.75
        u[2 * k, max(k - 1, 0)] += 0.25
        u[2 * k + 1, k] += 0.75
        u[2 * k + 1, min(k + 1, n - 1)] += 0.25
    return u


def constants():
    along_x = np.concatenate([banded(FX)] * 2, axis=0)
    along_y = np.concatenate([np.kron(np.eye(4), banded(FY))] * 2, axis=1)
    depth = np.zeros((FPS, SHOTS + 2))
    for k in range(SHOTS):
        depth[2 * k, k + 1] = 0.75
        depth[2 * k, k] = 0.25
        depth[2 * k + 1, k + 1] = 0.75
        depth[2 * k + 1, k + 2] = 0.25
    rows = doubling(CY)
    seven = np.eye(GROUP)
    up_y = np.concatenate(
        [np.kron(seven, rows[:, : CY // 2]), np.kron(seven, rows[:, CY // 2 :])], axis=1
    )
    down_zy = np.concatenate([np.kron(depth, rows[:, 0::2]), np.kron(depth, rows[:, 1::2])], axis=1).T
    eye = np.eye(CX)
    fold = np.zeros((2, 4, 4))
    for i, o in ((0, 0), (1, 2), (2, 1), (3, 3)):
        fold[0, i, o] = 1
    for i, o in ((0, 1), (3, 2)):
        fold[1, i, o] = 1
    fold = np.concatenate([np.kron(fold[0], eye), np.kron(fold[1], eye)], axis=0)
    up_x = np.kron(np.eye(2), doubling(CX).T)
    down_zy = np.stack(np.split(down_zy, 2, axis=1))
    out = (along_x, along_y, up_y, down_zy, up_x, up_x.T, fold)
    return [jnp.asarray(a.astype(jnp.bfloat16)) for a in out]


def dot(a, b, dims=((1,), (0,))):
    return lax.dot_general(a, b, (dims, ((), ())), preferred_element_type=F32)


def two(v):
    hi = v.astype(BF16)
    return hi, (v - hi.astype(F32)).astype(BF16)


def kernel(
    n,
    latent,
    w1_hbm,
    w2_hbm,
    head_hbm,
    wavelet_hbm,
    sources_hbm,
    receivers_hbm,
    along_x_hbm,
    along_y_hbm,
    up_x_hbm,
    up_xt_hbm,
    prev_hbm,
    cur_hbm,
    adj_hbm,
    up_y_hbm,
    up_zyt_hbm,
    fold_hbm,
    final_out,
    traces_out,
    gradient_out,
    head,
    w1,
    w2,
    wavelet,
    sources,
    receivers,
    along_x,
    along_y,
    up_x,
    up_xt,
    lap1,
    head_col,
    raw,
    fold,
    a1,
    a2,
    wp1,
    wp2,
    logits,
    vel,
    vels,
    f0,
    f1,
    f2,
    f3,
    f4,
    b1,
    b3,
    adj,
    up_y,
    up_zyt,
    speed,
    corr,
    pace,
    edge0,
    halo0,
    hot,
    seen,
    rec,
    recs,
    gr,
    grs,
    total,
    local_sem,
    lat_s,
    lat_r,
    hid_s,
    hid_r,
    rim_s,
    rim_r,
    vel_s,
    vel_r,
    rec_s,
    rec_r,
    gr_s,
    gr_r,
):
    me = lax.axis_index("slab")
    shot = lax.rem(me, SHOTS)
    slab = me // SHOTS
    slabs = n // SHOTS
    has_low = slab > 0
    has_high = slab < slabs - 1

    sends = (me < n - 1, me > 0)
    gets = (me > 0, me < n - 1)
    inner = pl.ds(2 * BLOCK, 4 * BLOCK)
    pairs = (
        (latent, raw.at[1]),
        (w1_hbm, w1),
        (cur_hbm, f1.at[inner]),
        (w2_hbm, w2),
        (receivers_hbm, receivers),
        (along_y_hbm, along_y),
        (along_x_hbm, along_x),
        (adj_hbm, adj),
        (up_x_hbm, up_x),
        (up_y_hbm, up_y),
        (wavelet_hbm, wavelet),
        (sources_hbm, sources),
        (prev_hbm, f0.at[inner]),
        (up_zyt_hbm, up_zyt),
        (up_xt_hbm, up_xt),
        (head_hbm, head),
        (fold_hbm, fold),
    )
    loads = [
        pltpu.make_async_copy(src, dst, local_sem.at[i]) for i, (src, dst) in enumerate(pairs)
    ]

    def remote(src, dst, send, recv, target):
        return pltpu.make_async_remote_copy(
            src_ref=src,
            dst_ref=dst,
            send_sem=send,
            recv_sem=recv,
            device_id={"slab": target},
            device_id_type=pl.DeviceIdType.MESH,
        )

    def peer(j):
        return lax.rem(me + j, n)

    barrier = pltpu.get_barrier_semaphore()

    def over_peers(what):
        def one(j, carry):
            what(j)
            return carry

        if n <= 16:
            for j in range(1, n):
                what(j)
        else:
            lax.fori_loop(1, n, one, 0)

    def greet(j):
        pl.semaphore_signal(
            barrier, inc=1, device_id={"slab": peer(j)}, device_id_type=pl.DeviceIdType.MESH
        )

    over_peers(greet)
    for load in loads:
        load.start()

    for a in (raw, a2):
        for side in range(2):

            @pl.when(jnp.logical_not(gets[side]))
            def _():
                a[2 * side] = jnp.zeros(a.shape[1:], BF16)

    pl.semaphore_wait(barrier, n - 1)

    def lat_copy(side, part, half):
        first, end = PAIRS[part]
        cols = pl.ds((first + half * COLS // 2) * 128, (end - first) * 128)
        return remote(
            latent.at[:, cols],
            raw.at[2 * side, :, cols],
            lat_s.at[side],
            lat_r.at[side, part],
            peer(1 if side == 0 else n - 1),
        )

    def arrived(ref, sem):
        remote(ref, ref, sem, sem, me).wait_recv()

    def departed(ref, sem):
        remote(ref, ref, sem, sem, me).wait_send()

    def hid_copy(side, piece):
        first, end = PIECES[piece]
        cols = pl.ds((first + 1) * 128, (end - first) * 128)
        return remote(
            a2.at[1, :, cols],
            a2.at[2 * side, :, cols],
            hid_s.at[side],
            hid_r.at[side, min(piece, 3)],
            peer(1 if side == 0 else n - 1),
        )

    def rim_copy(side, what):
        block = (5, 2)[side]
        to = (1, 6)[side]
        out, back = (4, 0) if side == 0 else (3, 7)
        if what == 0:
            src, dst = b1.at[pl.ds(block * BLOCK, BLOCK)], b1.at[pl.ds(to * BLOCK, BLOCK)]
        elif what == 1:
            src, dst = b1.at[pl.ds(out * BLOCK, BLOCK)], b1.at[pl.ds(back * BLOCK, BLOCK)]
        elif what == 2:
            src, dst = edge0.at[side], halo0.at[side]
        else:
            first, back = (4, 0) if side == 0 else (2, 6)
            src = b3.at[pl.ds(first * BLOCK, 2 * BLOCK)]
            dst = b3.at[pl.ds(back * BLOCK, 2 * BLOCK)]
        return remote(
            src,
            dst,
            rim_s.at[side, what // 3],
            rim_r.at[side, what // 3],
            peer(SHOTS if side == 0 else n - SHOTS),
        )

    rim_sends = (has_high, has_low)
    rim_gets = (has_low, has_high)

    def rows(b):
        return pl.ds(pl.multiple_of(b * BLOCK, BLOCK), BLOCK)

    def own(b):
        return pl.ds(pl.multiple_of((b - 2) * BLOCK, BLOCK), BLOCK)

    for part in range(len(PAIRS)):
        for side in range(2):

            @pl.when(sends[side])
            def _():
                lat_copy(side, part, 0).start()
                lat_copy(side, part, 1).start()

    loads[1].wait()
    loads[3].wait()
    for w, packed in ((w1, wp1), (w2, wp2)):
        for dx in range(3):
            packed[dx * CH : (dx + 1) * CH] = jnp.concatenate(
                [w[dz * 9 + dy * 3 + dx] for dy in range(3) for dz in range(3)], axis=1
            )

    for side in range(2):
        ext = (1, 6)[side]

        @pl.when(jnp.logical_not(rim_gets[side]))
        def _():
            for f in (f1, f2, f3, f4):
                f[ext * BLOCK : (ext + 1) * BLOCK] = jnp.zeros((BLOCK, FX), F32)

    loads[2].wait()
    loads[12].wait()
    b1[inner] = f1[inner].astype(BF16)
    edge0[0] = f0[5 * BLOCK : 6 * BLOCK].astype(BF16)
    edge0[1] = f0[2 * BLOCK : 3 * BLOCK].astype(BF16)
    loads[4].wait()
    loads[15].wait()
    station = receivers[:, shot]
    same = lax.broadcasted_iota(jnp.int32, (128, 128), 0) == lax.broadcasted_iota(
        jnp.int32, (128, 128), 1
    )

    def upright(v):
        return jnp.sum(
            jnp.where(same, jnp.broadcast_to(v.astype(F32), (128, 128)), 0.0), axis=1, keepdims=True
        ).astype(jnp.int32)

    station_row = upright((station[0:1] - slab * FPS) * FY + station[1:2])
    station_col = upright(station[2:3])
    row = lax.broadcasted_iota(jnp.int32, (128, BLOCK), 1)
    for b in range(4):
        hot[b] = (row + b * BLOCK == station_row).astype(F32).astype(BF16)
    at_col = lax.broadcasted_iota(jnp.int32, (128, FX), 1) == station_col
    seen[...] = jnp.zeros(seen.shape, F32)
    rec[...] = jnp.zeros((8, FX), F32)

    square = (CH, CH)
    diagonal = lax.broadcasted_iota(jnp.int32, square, 0) == lax.broadcasted_iota(
        jnp.int32, square, 1
    )
    spread = jnp.broadcast_to(head[...].astype(F32), square)
    head_col[...] = jnp.broadcast_to(
        jnp.sum(jnp.where(diagonal, spread, 0.0), axis=1, keepdims=True), (CH, 128)
    )

    lane = lax.broadcasted_iota(jnp.int32, (1, 128), 1)
    keep_left = lax.rem(lane, CX) > 0
    keep_right = lax.rem(lane, CX) < CX - 1

    def column(a, c):
        return a[:, :, c * 128 : (c + 1) * 128].reshape(3 * CH, 128)

    def put(a, c, v):
        a[:, :, c * 128 : (c + 1) * 128] = v.astype(BF16).reshape(3, CH, 128)

    def close(a):
        ends = jnp.concatenate([column(a, COLS), column(a, 1)], axis=1)
        moved = dot(ends, fold[256:])
        put(a, 0, moved[:, :128])
        put(a, COLS + 1, moved[:, 128:])

    def convolved(packed, a, columns):
        block = jnp.concatenate(
            [
                jnp.concatenate([column(a, j + dy) for dy in range(3)], axis=0)
                for j in columns
            ],
            axis=1,
        )
        taps = dot(packed[...], block)
        out = []
        for i in range(len(columns)):
            left, middle, right = (
                taps[dx * CH : (dx + 1) * CH, i * 128 : (i + 1) * 128] for dx in range(3)
            )
            v = (
                middle
                + jnp.where(keep_left, pltpu.roll(left, 1, 1), 0.0)
                + jnp.where(keep_right, pltpu.roll(right, 127, 1), 0.0)
            )
            out.append(jnp.where(v > 0, v, LEAK * v))
        return out

    loads[0].wait()
    loads[16].wait()

    def send_hidden(pieces):
        for side in range(2):

            @pl.when(sends[side])
            def _():
                for piece in pieces:
                    hid_copy(side, piece).start()

    for part, (first, end) in enumerate(PAIRS):
        for side in range(2):

            @pl.when(gets[side])
            def _():
                arrived(
                    raw.at[2 * side, :, pl.ds(0, 2 * (end - first) * 128)], lat_r.at[side, part]
                )

        for i in range(first, end):
            pair = jnp.concatenate([column(raw, i), column(raw, i + COLS // 2)], axis=1)
            folded = dot(pair, fold[:256])
            put(a1, 2 * i + 1, folded[:, :128])
            put(a1, 2 * i + 2, folded[:, 128:])
        if end == COLS // 2:
            close(a1)
        for j, v in zip(FIRST[part], convolved(wp1, a1, FIRST[part])):
            a2[1, :, (j + 1) * 128 : (j + 2) * 128] = v.astype(BF16)
        send_hidden((part, part + 1) if end == COLS // 2 else (part,))

    for what in range(3):
        for side in range(2):

            @pl.when(rim_sends[side])
            def _():
                rim_copy(side, what).start()

    def beside(now, c, planes):
        return now[pl.ds(pl.multiple_of(c * BLOCK + planes * FY, FY), BLOCK)]

    def laplace(now, blocks):
        centres = [now[rows(c)] for c in blocks]
        halves = [two(v) for v in centres]
        down = dot(
            along_y[...],
            jnp.concatenate([jnp.concatenate(h, axis=0) for h in halves], axis=1),
        )
        across = dot(
            jnp.concatenate([jnp.concatenate(h, axis=1) for h in halves], axis=0), along_x[...]
        )
        laps = []
        for i, (c, v) in enumerate(zip(blocks, centres)):
            lap = CENTRE * v + down[:, FX * i : FX * (i + 1)]
            lap = lap + across[BLOCK * i : BLOCK * (i + 1)]
            for k in range(1, 5):
                lap = lap + (SCALE * C[k]) * (beside(now, c, -k) + beside(now, c, k))
            laps.append(lap)
        return laps

    def advance(t, b, lap, v, before):
        pulse = jnp.where(linear == source_at - (b - 2) * (BLOCK * FX), wavelet[t - 1, shot], 0.0)
        return 2.0 * v - before + pace[rows(b)] * lap + pulse

    def weighted(t, b, lap):
        return adj[t - 1, own(b)].astype(F32) * lap

    def observe(t, b, new):
        hi, lo = two(new)
        got = dot(hot[b - 2], jnp.concatenate([hi, lo], axis=1))
        seen[t - 1] += got[:, :FX] + got[:, FX:]

    def finish(t, c, lap, now, before, new_f):
        new = advance(t, c, lap, now[rows(c)], before[rows(c)])
        new_f[(own if t == STEPS else rows)(c)] = new
        return new

    def step(t, blocks, now, before, new_f):
        for c, lap in zip(blocks, laplace(now, blocks)):
            finish(t, c, lap, now, before, new_f)
            corr[own(c)] += weighted(t, c, lap)

    for i in (5, 6, 7, 8, 9, 10, 11):
        loads[i].wait()
    source_at = (
        (sources[0, shot] - slab * FPS) * (FY * FX) + sources[1, shot] * FX + sources[2, shot]
    )
    linear = lax.broadcasted_iota(jnp.int32, (BLOCK, FX), 0) * FX + lax.broadcasted_iota(
        jnp.int32, (BLOCK, FX), 1
    )

    def first_laplace(blocks):
        for c, lap in zip(blocks, laplace(f1, blocks)):
            lap1[rows(c)] = lap
            corr[own(c)] = weighted(1, c, lap)

    first_laplace((3, 4))

    def get_hidden(piece):
        for side in range(2):

            @pl.when(gets[side])
            def _():
                arrived(a2.at[2 * side, :, pl.ds(128, 4 * 128)], hid_r.at[side, piece])

    for part, columns in enumerate(SECOND):
        get_hidden(part)
        if part == len(SECOND) - 1:
            close(a2)
        for j, v in zip(columns, convolved(wp2, a2, columns)):
            v = v * head_col[...]
            logits[8 * j : 8 * j + 8] = jnp.sum(v.reshape(CH // 8, 8, 128), axis=0)
    total_logits = jnp.sum(logits[...].reshape(COLS, 8, 128), axis=1)
    wave_speed = 1.5 + 3.0 / (1.0 + jnp.exp(-total_logits))
    vel[...] = wave_speed.astype(BF16)

    def vel_copy(k, to_slab, slot, send, recv):
        return remote(vel, vels.at[slot], vel_s.at[send], vel_r.at[recv], to_slab * SHOTS + k)

    lends_low = (shot <= 2) & has_low
    lends_high = (shot >= SHOTS - 3) & has_high

    def vel_sends():
        for j in range(1, SHOTS):
            vel_copy(lax.rem(shot + j, SHOTS), slab, shot + 3, 0, 0).start()

        @pl.when(lends_low)
        def _():
            for k in range(SHOTS):
                vel_copy(k, slab - 1, lax.rem(shot, 3) + 11, 1, 2).start()

        @pl.when(lends_high)
        def _():
            for k in range(SHOTS):
                vel_copy(k, slab + 1, lax.rem(shot + 1, 3), 1, 1).start()

    def vel_gets():
        arrived(vels.at[pl.ds(0, SHOTS - 1)], vel_r.at[0])
        for side in range(2):

            @pl.when(rim_gets[side])
            def _():
                arrived(vels.at[pl.ds(0, 3)], vel_r.at[side + 1])

    def rec_copy(j):
        return remote(rec, recs.at[j], rec_s.at[0], rec_r.at[0], peer(j))

    vel_sends()
    vels[shot + 3] = vel[...]
    for side in range(2):
        edge, ext = ((2, 1), (5, 6))[side]

        @pl.when(rim_gets[side])
        def _():
            arrived(b1.at[pl.ds(0, 3 * BLOCK)], rim_r.at[side, 0])

    first_laplace((2, 5))
    for side in range(2):
        ext = (1, 6)[side]

        @pl.when(rim_gets[side])
        def _():
            at = slice((0, 6)[side] * BLOCK, (2, 8)[side] * BLOCK)
            f1[at] = b1[at].astype(F32)
            f0[rows(ext)] = halo0[side].astype(F32)

    first_laplace((2, 5))
    for side in range(2):
        ext = (1, 6)[side]

        @pl.when(rim_gets[side])
        def _():
            lap1[rows(ext)] = laplace(f1, (ext,))[0]

    vel_gets()
    planes = []
    for i in range(2 * GROUP):
        plane = jnp.clip(slab * SHOTS - 3 + i, 0, n - 1)
        planes.append(vels[plane - slab * SHOTS + 3])
    wide = dot(jnp.concatenate(planes, axis=0), up_x[...])
    tall = []
    for g in range(2):
        part = wide[16 * GROUP * g : 16 * GROUP * (g + 1)]
        hi, lo = two(jnp.concatenate([part[:, :FX], part[:, FX:]], axis=0))
        both = dot(up_y[...], jnp.concatenate([hi, lo], axis=1))
        both = both[:, :FX] + both[:, FX:]
        tall += [both[FY * i : FY * (i + 1)] for i in range(GROUP)]
    for z in range(-4, FPS + 4):
        i = z // 2 + 3
        fine = 0.75 * tall[i] + 0.25 * tall[i + 1 if z % 2 else i - 1]
        at = z * FY + 2 * BLOCK
        if 0 <= z < FPS:
            speed[z * FY : (z + 1) * FY] = fine
        courant = COURANT * fine
        pace[at : at + FY] = courant * courant * (1.0 / SCALE)

    n1, n2 = jnp.where(has_low, 2, 5), jnp.where(has_low, 3, 4)
    g1, g2 = 7 - n1, 7 - n2
    far_too = has_low & has_high

    def second(c):
        finish(1, c, lap1[rows(c)], f1, f0, f2)

    for side in range(2):

        @pl.when(rim_gets[side])
        def _():
            second((1, 6)[side])

    for b in (2, 3, 4, 5):
        second(b)
    step(2, (n1, n2), f2, f1, f3)
    for c in (n1, n2):
        b3[rows(c)] = f3[rows(c)].astype(BF16)

    @pl.when(has_low)
    def _():
        rim_copy(1, 3).start()

    @pl.when(has_high & jnp.logical_not(has_low))
    def _():
        rim_copy(0, 3).start()

    step(2, (g1, g2), f2, f1, f3)

    @pl.when(far_too)
    def _():
        b3[4 * BLOCK : 6 * BLOCK] = f3[4 * BLOCK : 6 * BLOCK].astype(BF16)
        rim_copy(0, 3).start()

    for b in (2, 3, 4, 5):
        observe(1, b, f2[rows(b)])
        observe(2, b, f3[rows(b)])

    @pl.when(far_too)
    def _():
        rim_copy(1, 3).wait_recv()
        f3[6 * BLOCK :] = b3[6 * BLOCK :].astype(F32)
        finish(3, 6, laplace(f3, (6,))[0], f3, f2, f4)

    step(3, (g1, g2), f3, f2, f4)
    step(3, (n2,), f3, f2, f4)
    step(4, (g1, g2), f4, f3, final_out)
    for b in (g1, g2):
        observe(4, b, final_out[own(b)])
    for b in (g1, g2, n2):
        observe(3, b, f4[rows(b)])

    def collected(first):
        parts = []
        for t in (first, first + 1):
            parts += two(jnp.where(at_col, seen[t - 1], 0.0))
        wide = (8, 4 * FX)
        pick = lax.broadcasted_iota(jnp.int32, wide, 0) == first - 1 + lax.broadcasted_iota(
            jnp.int32, wide, 1
        ) // (2 * FX)
        rec[...] += dot(
            pick.astype(F32).astype(BF16), jnp.concatenate(parts, axis=1), ((1,), (1,))
        )

    collected(1)
    loads[13].wait()
    loads[14].wait()

    def raised(pair):
        at = pl.ds(pl.multiple_of(pair * 2 * BLOCK, 2 * BLOCK), 2 * BLOCK)
        fine = (2.0 * COURANT * COURANT / SCALE) * speed[at] * corr[at]
        return dot(up_zyt[pair], fine.astype(BF16))

    near_pair = jnp.where(has_low, 0, 1)
    tall = raised(1 - near_pair)
    @pl.when(has_low)
    def _():
        rim_copy(0, 3).wait_recv()

    @pl.when(has_high & jnp.logical_not(has_low))
    def _():
        rim_copy(1, 3).wait_recv()

    halo = pl.ds(pl.multiple_of(jnp.where(has_low, 0, 6 * BLOCK), 2 * BLOCK), 2 * BLOCK)
    ext = jnp.where(has_low, 1, 6)
    f3[halo] = b3[halo].astype(F32)
    lap_ext, lap = laplace(f3, (ext, n1))
    finish(3, ext, lap_ext, f3, f2, f4)
    finish(3, n1, lap, f3, f2, f4)
    corr[own(n1)] += weighted(3, n1, lap)
    step(4, (n1, n2), f4, f3, final_out)
    observe(3, n1, f4[rows(n1)])
    for b in (n1, n2):
        observe(4, b, final_out[own(b)])
    collected(3)
    tall = tall + raised(near_pair)
    half = tall.shape[0] // 2
    hi, lo = two(jnp.concatenate([tall[:half], tall[half:]], axis=1))
    narrow = dot(hi, up_xt[...]) + dot(lo, up_xt[...])
    gr[...] = narrow.reshape(SHOTS + 2, 16, FX)
    over_peers(lambda j: rec_copy(j).start())


    @pl.when(jnp.logical_not(has_low))
    def _():
        gr[1] += gr[0]

    @pl.when(jnp.logical_not(has_high))
    def _():
        gr[SHOTS] += gr[SHOTS + 1]

    def gr_copy(j):
        other = lax.rem(shot + j, SHOTS)
        return remote(
            gr.at[other + 1], grs.at[j], gr_s.at[0], gr_r.at[0], slab * SHOTS + other
        )

    def low_copy(slot):
        return remote(
            gr.at[0], grs.at[slot], gr_s.at[1], gr_r.at[1], lax.rem(slab * SHOTS - 1 + n, n)
        )

    def high_copy(slot):
        return remote(
            gr.at[SHOTS + 1],
            grs.at[slot],
            gr_s.at[2],
            gr_r.at[2],
            lax.rem((slab + 1) * SHOTS, n),
        )

    @pl.when(has_low)
    def _():
        low_copy(8 + shot).start()

    @pl.when(has_high)
    def _():
        high_copy(16 + shot).start()

    for j in range(1, SHOTS):
        gr_copy(j).start()


    recs[0] = rec[...]
    arrived(recs.at[pl.ds(1, n - 1)], rec_r.at[0])
    for s in range(SHOTS):

        def slab_term(k, acc):
            return acc + recs[lax.rem(me - (k * SHOTS + s) + n, n)]

        summed = lax.fori_loop(0, slabs, slab_term, jnp.zeros((8, FX), F32))
        traces_out[s] = summed[:STEPS]

    arrived(grs.at[pl.ds(1, SHOTS - 1)], gr_r.at[0])
    summed = gr[shot + 1]
    for j in range(1, SHOTS):
        summed = summed + grs[j]
    total[...] = summed

    @pl.when((shot == SHOTS - 1) & has_high)
    def _():
        arrived(grs.at[pl.ds(8, SHOTS)], gr_r.at[1])
        total[...] += jnp.sum(grs[8:16], axis=0)

    @pl.when((shot == 0) & has_low)
    def _():
        arrived(grs.at[pl.ds(16, SHOTS)], gr_r.at[2])
        total[...] += jnp.sum(grs[16:24], axis=0)

    gradient_out[...] = total[...]

    for side in range(2):

        @pl.when(sends[side])
        def _():
            departed(raw.at[0], lat_s.at[side])
            departed(a2.at[1, :, pl.ds(128, CELLS)], hid_s.at[side])

        @pl.when(rim_sends[side])
        def _():
            departed(b1.at[pl.ds(0, 3 * BLOCK)], rim_s.at[side, 0])
            departed(b3.at[pl.ds(0, 2 * BLOCK)], rim_s.at[side, 1])

    departed(vels.at[pl.ds(0, SHOTS - 1)], vel_s.at[0])

    @pl.when(lends_low | lends_high)
    def _():
        departed(vels.at[pl.ds(0, SHOTS)], vel_s.at[1])

    departed(recs.at[pl.ds(1, n - 1)], rec_s.at[0])
    departed(grs.at[pl.ds(1, SHOTS - 1)], gr_s.at[0])

    @pl.when(has_low)
    def _():
        departed(grs.at[0], gr_s.at[1])

    @pl.when(has_high)
    def _():
        departed(grs.at[0], gr_s.at[2])


def hand_over(a, b, c, x, y, z, sem):
    copies = [
        pltpu.make_async_copy(src, dst, sem.at[i])
        for i, (src, dst) in enumerate(((a, x), (b, y), (c, z)))
    ]
    for copy in copies:
        copy.start()
    for copy in copies:
        copy.wait()


def body(
    n,
    latent,
    conv1_weight,
    conv2_weight,
    head,
    p_prev,
    p_cur,
    adjoint,
    wavelet,
    sources,
    receivers,
):
    along_x, along_y, up_y, up_zyt, up_x, up_xt, fold = constants()
    vmem = pl.BlockSpec(memory_space=pltpu.VMEM)
    hbm = pl.BlockSpec(memory_space=pl.ANY)
    dma = pltpu.SemaphoreType.DMA
    final, traces, gradient = pl.pallas_call(
        functools.partial(kernel, n),
        out_shape=(
            pltpu.VMEM((FPS * FY, FX), F32),
            pltpu.VMEM((SHOTS, STEPS, 128), F32),
            pltpu.VMEM((16, FX), F32),
        ),
        in_specs=[hbm] * 17,
        out_specs=(vmem, vmem, vmem),
        scratch_shapes=[
            pltpu.VMEM((1, CH), BF16),
            pltpu.VMEM(conv1_weight.shape, BF16),
            pltpu.VMEM(conv2_weight.shape, BF16),
            pltpu.SMEM((STEPS, SHOTS), F32),
            pltpu.SMEM((3, SHOTS), jnp.int32),
            pltpu.VMEM((3, SHOTS, 128), jnp.int32),
            pltpu.VMEM(along_x.shape, BF16),
            pltpu.VMEM(along_y.shape, BF16),
            pltpu.VMEM(up_x.shape, BF16),
            pltpu.VMEM(up_xt.shape, BF16),
            pltpu.VMEM((WINDOW, FX), F32),
            pltpu.VMEM((CH, 128), F32),
            pltpu.VMEM((3, CH, CELLS), BF16),
            pltpu.VMEM(fold.shape, BF16),
            pltpu.VMEM((3, CH, (COLS + 2) * 128), BF16),
            pltpu.VMEM((3, CH, (COLS + 2) * 128), BF16),
            pltpu.VMEM((3 * CH, 9 * CH), BF16),
            pltpu.VMEM((3 * CH, 9 * CH), BF16),
            pltpu.VMEM((COLS * 8, 128), F32),
            pltpu.VMEM((16, FX), BF16),
            pltpu.VMEM((2 * GROUP, 16, FX), BF16),
            *[pltpu.VMEM((WINDOW, FX), F32)] * 5,
            *[pltpu.VMEM((WINDOW, FX), BF16)] * 2,
            pltpu.VMEM((STEPS, FPS * FY, FX), BF16),
            pltpu.VMEM(up_y.shape, BF16),
            pltpu.VMEM(up_zyt.shape, BF16),
            pltpu.VMEM((FPS * FY, FX), F32),
            pltpu.VMEM((FPS * FY, FX), F32),
            pltpu.VMEM((WINDOW, FX), F32),
            pltpu.VMEM((2, BLOCK, FX), BF16),
            pltpu.VMEM((2, BLOCK, FX), BF16),
            pltpu.VMEM((4, 128, BLOCK), BF16),
            pltpu.VMEM((STEPS, 128, FX), F32),
            pltpu.VMEM((8, FX), F32),
            pltpu.VMEM((n, 8, FX), F32),
            pltpu.VMEM((SHOTS + 2, 16, FX), F32),
            pltpu.VMEM((3 * SHOTS, 16, FX), F32),
            pltpu.VMEM((16, FX), F32),
            dma((18,)),
            dma((2,)),
            dma((2, 4)),
            dma((2,)),
            dma((2, 4)),
            dma((2, 2)),
            dma((2, 2)),
            dma((2,)),
            dma((3,)),
            dma((1,)),
            dma((1,)),
            dma((3,)),
            dma((3,)),
        ],
        compiler_params=pltpu.CompilerParams(
            collective_id=0, has_side_effects=True, vmem_limit_bytes=VMEM_BYTES
        ),
    )(
        latent.reshape(CH, CELLS),
        conv1_weight,
        conv2_weight,
        head.reshape(1, CH),
        wavelet.T,
        sources.T,
        receivers.transpose(1, 0, 2),
        along_x,
        along_y,
        up_x,
        up_xt,
        p_prev.reshape(FPS * FY, FX),
        p_cur.reshape(FPS * FY, FX),
        adjoint.reshape(STEPS, FPS * FY, FX),
        up_y,
        up_zyt,
        fold,
    )
    final, traces, gradient = pl.pallas_call(
        hand_over,
        out_shape=(
            jax.ShapeDtypeStruct((FPS * FY, FX), F32),
            jax.ShapeDtypeStruct((SHOTS, STEPS, 128), F32),
            jax.ShapeDtypeStruct((16, FX), F32),
        ),
        in_specs=[vmem] * 3,
        out_specs=[hbm] * 3,
        scratch_shapes=[dma((3,))],
    )(*[pltpu.with_memory_space_constraint(v, pltpu.VMEM) for v in (final, traces, gradient)])
    return final.reshape(1, FPS, FY, FX), traces, gradient.reshape(1, CELLS)


def solution(mesh):
    in_specs = (
        P(None, ("groups", "slab"), None),
        P(),
        P(),
        P(),
        P(("groups", "slab"), None, None, None),
        P(("groups", "slab"), None, None, None),
        P(None, ("groups", "slab"), None, None, None),
        P("groups", None),
        P("groups", None),
        P("groups", None, None),
    )
    out_specs = (
        P(("groups", "slab"), None, None, None),
        P("groups", None, None),
        P(("groups", "slab"), None),
    )
    return jax.shard_map(
        functools.partial(body, mesh.shape["slab"]),
        mesh=mesh,
        in_specs=in_specs,
        out_specs=out_specs,
        check_vma=False,
    )
```

time: 50.1 us -> 42 us (0.84)
  Pallas kernels: 49.3 us -> 41.2 us
    pallas_call x2, Pallas kernels: 49.3 us -> 41.2 us  [the longest x1 40.4 us: body(): pl.pallas_call(functools.partial(kernel, n), out_shape=(pltpu.VMEM((FPS *...]
where the time goes in v1:
time: 42 us; the launch traced here: 41.8 us
  Pallas kernels  41.2 us (98%)
  between operations  0.64 us (2%)
    pallas_call x1, Pallas kernels, body(): pl.pallas_call(functools.partial(kernel, n), out_shape=(pltpu.VMEM((FPS *...  40.4 us

profile of v1, /device:TPU:0, one launch (start us, length us, event | category | flops | bytes accessed | tf_op | source)
XLA Modules:
  0.0 41.8 jit_solution(14936438123113354854)
XLA Ops:
  0.6 40.4 %shard_map.184 = (f32[1024,128]{1,0:T(8,128)S(1)}, f32[8,4,128]{2,1,0:T(4,128)S(1)}, f32[16,128]{1,0:T(8,128)S(1)}) custom-call(bf16[64,2048]{1,0:T(8,128)(2,1)} %bitcast.13, bf16[27,64,64]{2,1,0:T(8,128)(2,1)} %w1_hbm.1, bf16[27,64,64]{2,1,0:T(8,128)(2,1)} %w2_hbm.1, bf16[1,64]{1,0:T(2,128)(2,1)} %bitcast.17, f32[4,8]{1,0:T(4,128)} %bitcast.15, ...), custom_call_target="tpu_custom_call" | custom-call | tf_op jit(solution)/shard_map/pallas_call | solution.py:832
  41.0 0.8 %shard_map.185 = (f32[1024,128]{1,0:T(8,128)}, f32[8,4,128]{2,1,0:T(4,128)}, f32[16,128]{1,0:T(8,128)}) custom-call(f32[1024,128]{1,0:T(8,128)S(1)} %get-tuple-element.9.a, f32[8,4,128]{2,1,0:T(4,128)S(1)} %get-tuple-element.10.b, f32[16,128]{1,0:T(8,128)S(1)} %get-tuple-element.11.c), custom_call_target="tpu_custom_call" | custom-call | tf_op jit(solution)/shard_map/pallas_call | solution.py:916

commit v2 on v1

--- a/solution.py
+++ b/solution.py
@@ -18,6 +18,8 @@
 FY = 64
 FX = 128
 VMEM_BYTES = 60 * 2**20
+RIMS_AT = (-1,3,4)
+HALVES = 1
 PAIRS = ((0, 3), (3, 5), (5, 7), (7, 8))
 FIRST = ((1, 2, 3, 4), (5, 6, 7, 8), (9, 10, 11, 12), (13, 14, 15, 0))
 PIECES = ((1, 5), (5, 9), (9, 13), (13, 16), (0, 1))
@@ -294,7 +296,7 @@
             src,
             dst,
             rim_s.at[side, what // 3],
-            rim_r.at[side, what // 3],
+            rim_r.at[side, (what + 1) // 2],
             peer(SHOTS if side == 0 else n - SHOTS),
         )
 
@@ -336,6 +338,16 @@
     b1[inner] = f1[inner].astype(BF16)
     edge0[0] = f0[5 * BLOCK : 6 * BLOCK].astype(BF16)
     edge0[1] = f0[2 * BLOCK : 3 * BLOCK].astype(BF16)
+    def give_rims(at):
+        for what in range(3):
+            for side in range(2):
+                if RIMS_AT[what] == at:
+
+                    @pl.when(rim_sends[side])
+                    def _():
+                        rim_copy(side, what).start()
+
+    give_rims(-1)
     loads[4].wait()
     loads[15].wait()
     station = receivers[:, shot]
@@ -355,7 +367,7 @@
         hot[b] = (row + b * BLOCK == station_row).astype(F32).astype(BF16)
     at_col = lax.broadcasted_iota(jnp.int32, (128, FX), 1) == station_col
     seen[...] = jnp.zeros(seen.shape, F32)
-    rec[...] = jnp.zeros((8, FX), F32)
+    rec[...] = jnp.zeros((STEPS, FX), F32)
 
     square = (CH, CH)
     diagonal = lax.broadcasted_iota(jnp.int32, square, 0) == lax.broadcasted_iota(
@@ -434,13 +446,7 @@
         for j, v in zip(FIRST[part], convolved(wp1, a1, FIRST[part])):
             a2[1, :, (j + 1) * 128 : (j + 2) * 128] = v.astype(BF16)
         send_hidden((part, part + 1) if end == COLS // 2 else (part,))
-
-    for what in range(3):
-        for side in range(2):
-
-            @pl.when(rim_sends[side])
-            def _():
-                rim_copy(side, what).start()
+        give_rims(part)
 
     def beside(now, c, planes):
         return now[pl.ds(pl.multiple_of(c * BLOCK + planes * FY, FY), BLOCK)]
@@ -500,6 +506,7 @@
             lap1[rows(c)] = lap
             corr[own(c)] = weighted(1, c, lap)
 
+    give_rims(4)
     first_laplace((3, 4))
 
     def get_hidden(piece):
@@ -558,24 +565,18 @@
 
         @pl.when(rim_gets[side])
         def _():
-            arrived(b1.at[pl.ds(0, 3 * BLOCK)], rim_r.at[side, 0])
+            arrived(b1.at[pl.ds(0, BLOCK)], rim_r.at[side, 0])
+            f1[rows((1, 6)[side])] = b1[rows((1, 6)[side])].astype(F32)
 
     first_laplace((2, 5))
     for side in range(2):
-        ext = (1, 6)[side]
+        ext, far = ((1, 0), (6, 7))[side]
 
         @pl.when(rim_gets[side])
         def _():
-            at = slice((0, 6)[side] * BLOCK, (2, 8)[side] * BLOCK)
-            f1[at] = b1[at].astype(F32)
+            arrived(b1.at[pl.ds(0, 2 * BLOCK)], rim_r.at[side, 1])
+            f1[rows(far)] = b1[rows(far)].astype(F32)
             f0[rows(ext)] = halo0[side].astype(F32)
-
-    first_laplace((2, 5))
-    for side in range(2):
-        ext = (1, 6)[side]
-
-        @pl.when(rim_gets[side])
-        def _():
             lap1[rows(ext)] = laplace(f1, (ext,))[0]
 
     vel_gets()
@@ -660,9 +661,10 @@
         pick = lax.broadcasted_iota(jnp.int32, wide, 0) == first - 1 + lax.broadcasted_iota(
             jnp.int32, wide, 1
         ) // (2 * FX)
-        rec[...] += dot(
+        line = dot(
             pick.astype(F32).astype(BF16), jnp.concatenate(parts, axis=1), ((1,), (1,))
         )
+        rec[...] += line[:STEPS]
 
     collected(1)
     loads[13].wait()
@@ -750,8 +752,8 @@
         def slab_term(k, acc):
             return acc + recs[lax.rem(me - (k * SHOTS + s) + n, n)]
 
-        summed = lax.fori_loop(0, slabs, slab_term, jnp.zeros((8, FX), F32))
-        traces_out[s] = summed[:STEPS]
+        summed = lax.fori_loop(0, slabs, slab_term, jnp.zeros((STEPS, FX), F32))
+        traces_out[s] = summed
 
     arrived(grs.at[pl.ds(1, SHOTS - 1)], gr_r.at[0])
     summed = gr[shot + 1]
@@ -802,10 +804,12 @@
 
 
 def hand_over(a, b, c, x, y, z, sem):
-    copies = [
-        pltpu.make_async_copy(src, dst, sem.at[i])
-        for i, (src, dst) in enumerate(((a, x), (b, y), (c, z)))
+    rows = FPS * FY // HALVES
+    parts = [
+        (a.at[pl.ds(i * rows, rows)], x.at[pl.ds(i * rows, rows)]) for i in range(HALVES)
     ]
+    parts += [(b, y), (c, z)]
+    copies = [pltpu.make_async_copy(src, dst, sem.at[i]) for i, (src, dst) in enumerate(parts)]
     for copy in copies:
         copy.start()
     for copy in copies:
@@ -872,8 +876,8 @@
             pltpu.VMEM((2, BLOCK, FX), BF16),
             pltpu.VMEM((4, 128, BLOCK), BF16),
             pltpu.VMEM((STEPS, 128, FX), F32),
-            pltpu.VMEM((8, FX), F32),
-            pltpu.VMEM((n, 8, FX), F32),
+            pltpu.VMEM((STEPS, FX), F32),
+            pltpu.VMEM((n, STEPS, FX), F32),
             pltpu.VMEM((SHOTS + 2, 16, FX), F32),
             pltpu.VMEM((3 * SHOTS, 16, FX), F32),
             pltpu.VMEM((16, FX), F32),
@@ -883,7 +887,7 @@
             dma((2,)),
             dma((2, 4)),
             dma((2, 2)),
-            dma((2, 2)),
+            dma((2, 3)),
             dma((2,)),
             dma((3,)),
             dma((1,)),
@@ -922,7 +926,7 @@
         ),
         in_specs=[vmem] * 3,
         out_specs=[hbm] * 3,
-        scratch_shapes=[dma((3,))],
+        scratch_shapes=[dma((HALVES + 2,))],
     )(*[pltpu.with_memory_space_constraint(v, pltpu.VMEM) for v in (final, traces, gradient)])
     return final.reshape(1, FPS, FY, FX), traces, gradient.reshape(1, CELLS)
 

time: 42 us -> 40.7 us (0.969)
  Pallas kernels: 41.2 us -> 39.9 us
    pallas_call x1, Pallas kernels: 40.4 us -> 39 us  [body(): pl.pallas_call(functools.partial(kernel, n), out_shape=(pltpu.VMEM((FPS *...]
where the time goes in v2:
time: 40.7 us; the launch traced here: 40.5 us
  Pallas kernels  39.9 us (98%)
  between operations  0.64 us (2%)
    pallas_call x1, Pallas kernels, body(): pl.pallas_call(functools.partial(kernel, n), out_shape=(pltpu.VMEM((FPS *...  39 us
    pallas_call x1, Pallas kernels, body(): pl.pallas_call(hand_over, out_shape=(jax.ShapeDtypeStruct((FPS * FY, FX),...  0.83 us

profile of v2, /device:TPU:0, one launch (start us, length us, event | category | flops | bytes accessed | tf_op | source)
XLA Modules:
  0.0 40.5 jit_solution(387390292032378694)
XLA Ops:
  0.6 39.0 %shard_map.184 = (f32[1024,128]{1,0:T(8,128)S(1)}, f32[8,4,128]{2,1,0:T(4,128)S(1)}, f32[16,128]{1,0:T(8,128)S(1)}) custom-call(bf16[64,2048]{1,0:T(8,128)(2,1)} %bitcast.13, bf16[27,64,64]{2,1,0:T(8,128)(2,1)} %w1_hbm.1, bf16[27,64,64]{2,1,0:T(8,128)(2,1)} %w2_hbm.1, bf16[1,64]{1,0:T(2,128)(2,1)} %bitcast.17, f32[4,8]{1,0:T(4,128)} %bitcast.15, ...), custom_call_target="tpu_custom_call" | custom-call | tf_op jit(solution)/shard_map/pallas_call | solution.py:836
  39.7 0.8 %shard_map.185 = (f32[1024,128]{1,0:T(8,128)}, f32[8,4,128]{2,1,0:T(4,128)}, f32[16,128]{1,0:T(8,128)}) custom-call(f32[1024,128]{1,0:T(8,128)S(1)} %get-tuple-element.9.a, f32[8,4,128]{2,1,0:T(4,128)S(1)} %get-tuple-element.10.b, f32[16,128]{1,0:T(8,128)S(1)} %get-tuple-element.11.c), custom_call_target="tpu_custom_call" | custom-call | tf_op jit(solution)/shard_map/pallas_call | solution.py:920

commit v3 on v2

--- a/solution.py
+++ b/solution.py
@@ -18,7 +18,8 @@
 FY = 64
 FX = 128
 VMEM_BYTES = 60 * 2**20
-RIMS_AT = (-1,3,4)
+WHATS = (0, 1, 2, 4, 5)
+RIMS_AT = ((-1, 4,4,6,6), (-1, 4,6,7,7))
 HALVES = 1
 PAIRS = ((0, 3), (3, 5), (5, 7), (7, 8))
 FIRST = ((1, 2, 3, 4), (5, 6, 7, 8), (9, 10, 11, 12), (13, 14, 15, 0))
@@ -28,8 +29,10 @@
 
 C = (-205.0 / 72.0, 8.0 / 5.0, -1.0 / 5.0, 8.0 / 315.0, -1.0 / 560.0)
 BLOCK = 4 * FY
-WINDOW = 8 * BLOCK
-GROUP = 7
+OWN = 3
+WINDOW = (2 * OWN + 4) * BLOCK
+GROUP = 6
+REACH = 5
 SCALE = 5040.0
 CENTRE = 3.0 * SCALE * C[0]
 COURANT = 0.088
@@ -67,20 +70,18 @@
         depth[2 * k + 1, k + 1] = 0.75
         depth[2 * k + 1, k + 2] = 0.25
     rows = doubling(CY)
-    seven = np.eye(GROUP)
+    each = np.eye(GROUP)
     up_y = np.concatenate(
-        [np.kron(seven, rows[:, : CY // 2]), np.kron(seven, rows[:, CY // 2 :])], axis=1
+        [np.kron(each, rows[:, : CY // 2]), np.kron(each, rows[:, CY // 2 :])], axis=1
     )
     down_zy = np.concatenate([np.kron(depth, rows[:, 0::2]), np.kron(depth, rows[:, 1::2])], axis=1).T
     eye = np.eye(CX)
-    fold = np.zeros((2, 4, 4))
+    fold = np.zeros((4, 4))
     for i, o in ((0, 0), (1, 2), (2, 1), (3, 3)):
-        fold[0, i, o] = 1
-    for i, o in ((0, 1), (3, 2)):
-        fold[1, i, o] = 1
-    fold = np.concatenate([np.kron(fold[0], eye), np.kron(fold[1], eye)], axis=0)
+        fold[i, o] = 1
+    fold = np.kron(fold, eye)
     up_x = np.kron(np.eye(2), doubling(CX).T)
-    down_zy = np.stack(np.split(down_zy, 2, axis=1))
+    down_zy = np.stack(np.split(down_zy, 4, axis=1))
     out = (along_x, along_y, up_y, down_zy, up_x, up_x.T, fold)
     return [jnp.asarray(a.astype(jnp.bfloat16)) for a in out]
 
@@ -134,6 +135,7 @@
     a2,
     wp1,
     wp2,
+    taps,
     logits,
     vel,
     vels,
@@ -142,6 +144,8 @@
     f2,
     f3,
     f4,
+    f5,
+    f6,
     b1,
     b3,
     adj,
@@ -182,7 +186,7 @@
 
     sends = (me < n - 1, me > 0)
     gets = (me > 0, me < n - 1)
-    inner = pl.ds(2 * BLOCK, 4 * BLOCK)
+    inner = pl.ds(OWN * BLOCK, 4 * BLOCK)
     pairs = (
         (latent, raw.at[1]),
         (w1_hbm, w1),
@@ -279,24 +283,18 @@
         )
 
     def rim_copy(side, what):
-        block = (5, 2)[side]
-        to = (1, 6)[side]
-        out, back = (4, 0) if side == 0 else (3, 7)
-        if what == 0:
-            src, dst = b1.at[pl.ds(block * BLOCK, BLOCK)], b1.at[pl.ds(to * BLOCK, BLOCK)]
-        elif what == 1:
-            src, dst = b1.at[pl.ds(out * BLOCK, BLOCK)], b1.at[pl.ds(back * BLOCK, BLOCK)]
-        elif what == 2:
-            src, dst = edge0.at[side], halo0.at[side]
+        if what in (2, 5):
+            src, dst = edge0.at[side, what // 3], halo0.at[side, what // 3]
         else:
-            first, back = (4, 0) if side == 0 else (2, 6)
-            src = b3.at[pl.ds(first * BLOCK, 2 * BLOCK)]
-            dst = b3.at[pl.ds(back * BLOCK, 2 * BLOCK)]
+            b, deep = {0: (b1, 0), 1: (b1, 1), 3: (b3, 1), 4: (b1, 2)}[what]
+            block = (6 - deep, 3 + deep)[side]
+            to = (2 - deep, 7 + deep)[side]
+            src, dst = b.at[pl.ds(block * BLOCK, BLOCK)], b.at[pl.ds(to * BLOCK, BLOCK)]
         return remote(
             src,
             dst,
-            rim_s.at[side, what // 3],
-            rim_r.at[side, (what + 1) // 2],
+            rim_s.at[side, (0, 0, 0, 1, 2, 2)[what]],
+            rim_r.at[side, (0, 1, 1, 2, 3, 3)[what]],
             peer(SHOTS if side == 0 else n - SHOTS),
         )
 
@@ -307,7 +305,7 @@
         return pl.ds(pl.multiple_of(b * BLOCK, BLOCK), BLOCK)
 
     def own(b):
-        return pl.ds(pl.multiple_of((b - 2) * BLOCK, BLOCK), BLOCK)
+        return pl.ds(pl.multiple_of((b - OWN) * BLOCK, BLOCK), BLOCK)
 
     for part in range(len(PAIRS)):
         for side in range(2):
@@ -320,32 +318,45 @@
     loads[1].wait()
     loads[3].wait()
     for w, packed in ((w1, wp1), (w2, wp2)):
-        for dx in range(3):
-            packed[dx * CH : (dx + 1) * CH] = jnp.concatenate(
-                [w[dz * 9 + dy * 3 + dx] for dy in range(3) for dz in range(3)], axis=1
+        for tap in range(9):
+            packed[tap * CH : (tap + 1) * CH] = jnp.concatenate(
+                [w[dz * 9 + tap] for dz in range(3)], axis=1
             )
 
     for side in range(2):
-        ext = (1, 6)[side]
+        ext = (2, 7)[side]
 
         @pl.when(jnp.logical_not(rim_gets[side]))
         def _():
-            for f in (f1, f2, f3, f4):
+            for f in (f1, f2, f3):
                 f[ext * BLOCK : (ext + 1) * BLOCK] = jnp.zeros((BLOCK, FX), F32)
+
+    for f, empty in ((f3, (1, 8)), (f4, (2, 7))):
+        for b in empty:
+            f[rows(b)] = jnp.zeros((BLOCK, FX), F32)
+
+    for f in (f5, f6):
+        f[...] = jnp.zeros(f.shape, F32)
 
     loads[2].wait()
     loads[12].wait()
     b1[inner] = f1[inner].astype(BF16)
-    edge0[0] = f0[5 * BLOCK : 6 * BLOCK].astype(BF16)
-    edge0[1] = f0[2 * BLOCK : 3 * BLOCK].astype(BF16)
+    for side in range(2):
+        for deep in range(2):
+            edge0[side, deep] = f0[rows((6 - deep, 3 + deep)[side])].astype(BF16)
+
+    middle = (slab == 0) == (shot >= SHOTS // 2)
+
     def give_rims(at):
-        for what in range(3):
+        for times, mine in zip(RIMS_AT, (middle, jnp.logical_not(middle))):
+            whats = [what for what, t in zip(WHATS, times) if t == at]
             for side in range(2):
-                if RIMS_AT[what] == at:
-
-                    @pl.when(rim_sends[side])
+                if whats:
+
+                    @pl.when(rim_sends[side] & mine)
                     def _():
-                        rim_copy(side, what).start()
+                        for what in whats:
+                            rim_copy(side, what).start()
 
     give_rims(-1)
     loads[4].wait()
@@ -388,33 +399,33 @@
     def put(a, c, v):
         a[:, :, c * 128 : (c + 1) * 128] = v.astype(BF16).reshape(3, CH, 128)
 
-    def close(a):
-        ends = jnp.concatenate([column(a, COLS), column(a, 1)], axis=1)
-        moved = dot(ends, fold[256:])
-        put(a, 0, moved[:, :128])
-        put(a, COLS + 1, moved[:, 128:])
-
-    def convolved(packed, a, columns):
-        block = jnp.concatenate(
-            [
-                jnp.concatenate([column(a, j + dy) for dy in range(3)], axis=0)
-                for j in columns
-            ],
-            axis=1,
-        )
-        taps = dot(packed[...], block)
-        out = []
-        for i in range(len(columns)):
-            left, middle, right = (
-                taps[dx * CH : (dx + 1) * CH, i * 128 : (i + 1) * 128] for dx in range(3)
-            )
-            v = (
-                middle
-                + jnp.where(keep_left, pltpu.roll(left, 1, 1), 0.0)
-                + jnp.where(keep_right, pltpu.roll(right, 127, 1), 0.0)
-            )
-            out.append(jnp.where(v > 0, v, LEAK * v))
-        return out
+    low_half = lane < CX
+
+    def spread(packed, a, columns):
+        block = jnp.concatenate([column(a, j + 1) for j in columns], axis=1)
+        got = dot(packed[...], block)
+        for i, j in enumerate(columns):
+            taps[j] = got[:, i * 128 : (i + 1) * 128].reshape(9, CH, 128)
+
+    def gathered(j):
+        sums = []
+        for dx in range(3):
+            v = taps[j, 3 + dx]
+            if j > 0:
+                v = v + taps[j - 1, dx]
+            else:
+                v = v + jnp.where(low_half, 0.0, pltpu.roll(taps[COLS - 1, dx], CX, 1))
+            if j < COLS - 1:
+                v = v + taps[j + 1, 6 + dx]
+            else:
+                v = v + jnp.where(low_half, pltpu.roll(taps[0, 6 + dx], CX, 1), 0.0)
+            sums.append(v)
+        v = (
+            sums[1]
+            + jnp.where(keep_left, pltpu.roll(sums[0], 1, 1), 0.0)
+            + jnp.where(keep_right, pltpu.roll(sums[2], 127, 1), 0.0)
+        )
+        return jnp.where(v > 0, v, LEAK * v)
 
     loads[0].wait()
     loads[16].wait()
@@ -438,18 +449,23 @@
 
         for i in range(first, end):
             pair = jnp.concatenate([column(raw, i), column(raw, i + COLS // 2)], axis=1)
-            folded = dot(pair, fold[:256])
+            folded = dot(pair, fold[...])
             put(a1, 2 * i + 1, folded[:, :128])
             put(a1, 2 * i + 2, folded[:, 128:])
-        if end == COLS // 2:
-            close(a1)
-        for j, v in zip(FIRST[part], convolved(wp1, a1, FIRST[part])):
-            a2[1, :, (j + 1) * 128 : (j + 2) * 128] = v.astype(BF16)
+        spread(wp1, a1, range(2 * first, 2 * end))
+        for j in FIRST[part]:
+            a2[1, :, (j + 1) * 128 : (j + 2) * 128] = gathered(j).astype(BF16)
         send_hidden((part, part + 1) if end == COLS // 2 else (part,))
         give_rims(part)
 
     def beside(now, c, planes):
         return now[pl.ds(pl.multiple_of(c * BLOCK + planes * FY, FY), BLOCK)]
+
+    def in_depth(now, c):
+        lap = (SCALE * C[1]) * (beside(now, c, -1) + beside(now, c, 1))
+        for k in range(2, 5):
+            lap = lap + (SCALE * C[k]) * (beside(now, c, -k) + beside(now, c, k))
+        return lap
 
     def laplace(now, blocks):
         centres = [now[rows(c)] for c in blocks]
@@ -465,13 +481,11 @@
         for i, (c, v) in enumerate(zip(blocks, centres)):
             lap = CENTRE * v + down[:, FX * i : FX * (i + 1)]
             lap = lap + across[BLOCK * i : BLOCK * (i + 1)]
-            for k in range(1, 5):
-                lap = lap + (SCALE * C[k]) * (beside(now, c, -k) + beside(now, c, k))
-            laps.append(lap)
+            laps.append(lap + in_depth(now, c))
         return laps
 
     def advance(t, b, lap, v, before):
-        pulse = jnp.where(linear == source_at - (b - 2) * (BLOCK * FX), wavelet[t - 1, shot], 0.0)
+        pulse = jnp.where(linear == source_at - (b - OWN) * (BLOCK * FX), wavelet[t - 1, shot], 0.0)
         return 2.0 * v - before + pace[rows(b)] * lap + pulse
 
     def weighted(t, b, lap):
@@ -479,7 +493,7 @@
 
     def observe(t, b, new):
         hi, lo = two(new)
-        got = dot(hot[b - 2], jnp.concatenate([hi, lo], axis=1))
+        got = dot(hot[b - OWN], jnp.concatenate([hi, lo], axis=1))
         seen[t - 1] += got[:, :FX] + got[:, FX:]
 
     def finish(t, c, lap, now, before, new_f):
@@ -507,7 +521,7 @@
             corr[own(c)] = weighted(1, c, lap)
 
     give_rims(4)
-    first_laplace((3, 4))
+    first_laplace((4, 5))
 
     def get_hidden(piece):
         for side in range(2):
@@ -518,11 +532,11 @@
 
     for part, columns in enumerate(SECOND):
         get_hidden(part)
-        if part == len(SECOND) - 1:
-            close(a2)
-        for j, v in zip(columns, convolved(wp2, a2, columns)):
-            v = v * head_col[...]
+        spread(wp2, a2, FIRST[part])
+        for j in columns:
+            v = gathered(j) * head_col[...]
             logits[8 * j : 8 * j + 8] = jnp.sum(v.reshape(CH // 8, 8, 128), axis=0)
+    give_rims(5)
     total_logits = jnp.sum(logits[...].reshape(COLS, 8, 128), axis=1)
     wave_speed = 1.5 + 3.0 / (1.0 + jnp.exp(-total_logits))
     vel[...] = wave_speed.astype(BF16)
@@ -530,22 +544,22 @@
     def vel_copy(k, to_slab, slot, send, recv):
         return remote(vel, vels.at[slot], vel_s.at[send], vel_r.at[recv], to_slab * SHOTS + k)
 
-    lends_low = (shot <= 2) & has_low
-    lends_high = (shot >= SHOTS - 3) & has_high
+    lends_low = (shot < REACH) & has_low
+    lends_high = (shot >= SHOTS - REACH) & has_high
 
     def vel_sends():
         for j in range(1, SHOTS):
-            vel_copy(lax.rem(shot + j, SHOTS), slab, shot + 3, 0, 0).start()
+            vel_copy(lax.rem(shot + j, SHOTS), slab, shot + REACH, 0, 0).start()
 
         @pl.when(lends_low)
         def _():
             for k in range(SHOTS):
-                vel_copy(k, slab - 1, lax.rem(shot, 3) + 11, 1, 2).start()
+                vel_copy(k, slab - 1, lax.rem(shot, REACH) + SHOTS + REACH, 1, 2).start()
 
         @pl.when(lends_high)
         def _():
             for k in range(SHOTS):
-                vel_copy(k, slab + 1, lax.rem(shot + 1, 3), 1, 1).start()
+                vel_copy(k, slab + 1, lax.rem(shot + 2, REACH), 2, 1).start()
 
     def vel_gets():
         arrived(vels.at[pl.ds(0, SHOTS - 1)], vel_r.at[0])
@@ -553,111 +567,86 @@
 
             @pl.when(rim_gets[side])
             def _():
-                arrived(vels.at[pl.ds(0, 3)], vel_r.at[side + 1])
+                arrived(vels.at[pl.ds(0, REACH)], vel_r.at[side + 1])
 
     def rec_copy(j):
         return remote(rec, recs.at[j], rec_s.at[0], rec_r.at[0], peer(j))
 
     vel_sends()
-    vels[shot + 3] = vel[...]
+    vels[shot + REACH] = vel[...]
+    give_rims(6)
     for side in range(2):
-        edge, ext = ((2, 1), (5, 6))[side]
-
         @pl.when(rim_gets[side])
         def _():
+            ext = (2, 7)[side]
             arrived(b1.at[pl.ds(0, BLOCK)], rim_r.at[side, 0])
-            f1[rows((1, 6)[side])] = b1[rows((1, 6)[side])].astype(F32)
-
-    first_laplace((2, 5))
-    for side in range(2):
-        ext, far = ((1, 0), (6, 7))[side]
-
-        @pl.when(rim_gets[side])
-        def _():
-            arrived(b1.at[pl.ds(0, 2 * BLOCK)], rim_r.at[side, 1])
-            f1[rows(far)] = b1[rows(far)].astype(F32)
-            f0[rows(ext)] = halo0[side].astype(F32)
-            lap1[rows(ext)] = laplace(f1, (ext,))[0]
-
+            f1[rows(ext)] = b1[rows(ext)].astype(F32)
+
+    first_laplace((3, 6))
     vel_gets()
+    give_rims(7)
     planes = []
-    for i in range(2 * GROUP):
-        plane = jnp.clip(slab * SHOTS - 3 + i, 0, n - 1)
-        planes.append(vels[plane - slab * SHOTS + 3])
+    for i in range(3 * GROUP):
+        plane = jnp.clip(slab * SHOTS - REACH + i, 0, n - 1)
+        planes.append(vels[plane - slab * SHOTS + REACH])
     wide = dot(jnp.concatenate(planes, axis=0), up_x[...])
     tall = []
-    for g in range(2):
+    for g in range(3):
         part = wide[16 * GROUP * g : 16 * GROUP * (g + 1)]
         hi, lo = two(jnp.concatenate([part[:, :FX], part[:, FX:]], axis=0))
         both = dot(up_y[...], jnp.concatenate([hi, lo], axis=1))
         both = both[:, :FX] + both[:, FX:]
         tall += [both[FY * i : FY * (i + 1)] for i in range(GROUP)]
-    for z in range(-4, FPS + 4):
-        i = z // 2 + 3
+    for z in range(-8, FPS + 8):
+        i = z // 2 + REACH
         fine = 0.75 * tall[i] + 0.25 * tall[i + 1 if z % 2 else i - 1]
-        at = z * FY + 2 * BLOCK
+        at = z * FY + OWN * BLOCK
         if 0 <= z < FPS:
             speed[z * FY : (z + 1) * FY] = fine
         courant = COURANT * fine
         pace[at : at + FY] = courant * courant * (1.0 / SCALE)
 
-    n1, n2 = jnp.where(has_low, 2, 5), jnp.where(has_low, 3, 4)
-    g1, g2 = 7 - n1, 7 - n2
+    n1, n2 = jnp.where(has_low, 3, 6), jnp.where(has_low, 4, 5)
+    g1, g2 = 9 - n1, 9 - n2
     far_too = has_low & has_high
 
     def second(c):
         finish(1, c, lap1[rows(c)], f1, f0, f2)
 
+    for b in (3, 4, 5, 6):
+        second(b)
+    step(2, (n2, g2), f2, f1, f3)
+    for c in (4, 5):
+        b3[rows(c)] = f3[rows(c)].astype(BF16)
     for side in range(2):
 
-        @pl.when(rim_gets[side])
+        @pl.when(rim_sends[side])
         def _():
-            second((1, 6)[side])
-
-    for b in (2, 3, 4, 5):
-        second(b)
-    step(2, (n1, n2), f2, f1, f3)
-    for c in (n1, n2):
-        b3[rows(c)] = f3[rows(c)].astype(BF16)
-
-    @pl.when(has_low)
-    def _():
-        rim_copy(1, 3).start()
-
-    @pl.when(has_high & jnp.logical_not(has_low))
-    def _():
-        rim_copy(0, 3).start()
-
-    step(2, (g1, g2), f2, f1, f3)
-
+            rim_copy(side, 3).start()
+
+    def deeper(side):
+        ext, far, last = ((2, 1, 0), (7, 8, 9))[side]
+        arrived(b1.at[pl.ds(0, 2 * BLOCK)], rim_r.at[side, 1])
+        arrived(b1.at[pl.ds(0, 2 * BLOCK)], rim_r.at[side, 3])
+        for c in (far, last):
+            f1[rows(c)] = b1[rows(c)].astype(F32)
+        for i, c in enumerate((ext, far)):
+            f0[rows(c)] = halo0[side, i].astype(F32)
+        for c, lap in zip((ext, far), laplace(f1, (ext, far))):
+            finish(1, c, lap, f1, f0, f2)
+        finish(2, ext, laplace(f2, (ext,))[0], f2, f1, f3)
+
+    give_rims(8)
     @pl.when(far_too)
     def _():
-        b3[4 * BLOCK : 6 * BLOCK] = f3[4 * BLOCK : 6 * BLOCK].astype(BF16)
-        rim_copy(0, 3).start()
-
-    for b in (2, 3, 4, 5):
-        observe(1, b, f2[rows(b)])
-        observe(2, b, f3[rows(b)])
-
-    @pl.when(far_too)
-    def _():
-        rim_copy(1, 3).wait_recv()
-        f3[6 * BLOCK :] = b3[6 * BLOCK :].astype(F32)
-        finish(3, 6, laplace(f3, (6,))[0], f3, f2, f4)
-
-    step(3, (g1, g2), f3, f2, f4)
-    step(3, (n2,), f3, f2, f4)
-    step(4, (g1, g2), f4, f3, final_out)
-    for b in (g1, g2):
-        observe(4, b, final_out[own(b)])
-    for b in (g1, g2, n2):
-        observe(3, b, f4[rows(b)])
-
-    def collected(first):
+        deeper(1)
+
+    step(2, (g1,), f2, f1, f3)
+    def collected(first, last):
         parts = []
-        for t in (first, first + 1):
+        for t in range(first, last + 1):
             parts += two(jnp.where(at_col, seen[t - 1], 0.0))
-        wide = (8, 4 * FX)
+        wide = (8, (last - first + 1) * 2 * FX)
         pick = lax.broadcasted_iota(jnp.int32, wide, 0) == first - 1 + lax.broadcasted_iota(
             jnp.int32, wide, 1
         ) // (2 * FX)
@@ -666,17 +655,45 @@
         )
         rec[...] += line[:STEPS]
 
-    collected(1)
+    for b in (3, 4, 5, 6):
+        observe(1, b, f2[rows(b)])
+    for b in (g1, g2, n2):
+        observe(2, b, f3[rows(b)])
+    collected(1, 1)
+
+    @pl.when(far_too)
+    def _():
+        rim_copy(1, 3).wait_recv()
+        f3[rows(8)] = b3[rows(8)].astype(F32)
+        finish(3, 7, laplace(f3, (7,))[0], f3, f2, f4)
+
+    step(3, (g1, g2), f3, f2, f4)
+    step(4, (g1,), f4, f3, final_out)
+    for b in (g1, g2):
+        observe(3, b, f4[rows(b)])
+    observe(4, g1, final_out[own(g1)])
     loads[13].wait()
     loads[14].wait()
 
-    def raised(pair):
-        at = pl.ds(pl.multiple_of(pair * 2 * BLOCK, 2 * BLOCK), 2 * BLOCK)
-        fine = (2.0 * COURANT * COURANT / SCALE) * speed[at] * corr[at]
-        return dot(up_zyt[pair], fine.astype(BF16))
-
-    near_pair = jnp.where(has_low, 0, 1)
-    tall = raised(1 - near_pair)
+    def raised(c):
+        fine = (2.0 * COURANT * COURANT / SCALE) * speed[own(c)] * corr[own(c)]
+        return dot(up_zyt[c - OWN], fine.astype(BF16))
+
+    ext, far = jnp.where(has_low, 2, 7), jnp.where(has_low, 1, 8)
+    pl.when(has_low)(lambda: deeper(0))
+    pl.when(has_high & jnp.logical_not(has_low))(lambda: deeper(1))
+    step(2, (n1,), f2, f1, f3)
+    step(3, (n2, n1), f3, f2, f4)
+    step(4, (g2, n2), f4, f3, final_out)
+    lap1[rows(ext)] = laplace(f3, (ext,))[0]
+    lap1[rows(n1)] = laplace(f4, (n1,))[0]
+    observe(2, n1, f3[rows(n1)])
+    for b in (n2, n1):
+        observe(3, b, f4[rows(b)])
+    for b in (g2, n2):
+        observe(4, b, final_out[own(b)])
+    collected(2, 3)
+    tall = raised(g1) + raised(g2) + raised(n2)
     @pl.when(has_low)
     def _():
         rim_copy(0, 3).wait_recv()
@@ -685,19 +702,15 @@
     def _():
         rim_copy(1, 3).wait_recv()
 
-    halo = pl.ds(pl.multiple_of(jnp.where(has_low, 0, 6 * BLOCK), 2 * BLOCK), 2 * BLOCK)
-    ext = jnp.where(has_low, 1, 6)
-    f3[halo] = b3[halo].astype(F32)
-    lap_ext, lap = laplace(f3, (ext, n1))
-    finish(3, ext, lap_ext, f3, f2, f4)
-    finish(3, n1, lap, f3, f2, f4)
-    corr[own(n1)] += weighted(3, n1, lap)
-    step(4, (n1, n2), f4, f3, final_out)
-    observe(3, n1, f4[rows(n1)])
-    for b in (n1, n2):
-        observe(4, b, final_out[own(b)])
-    collected(3)
-    tall = tall + raised(near_pair)
+    f5[rows(far)] = b3[rows(far)].astype(F32)
+    lap = lap1[rows(ext)] + in_depth(f5, ext)
+    f6[rows(ext)] = advance(3, ext, lap, f3[rows(ext)], f2[rows(ext)])
+    lap = lap1[rows(n1)] + in_depth(f6, n1)
+    last = finish(4, n1, lap, f4, f3, final_out)
+    corr[own(n1)] += weighted(4, n1, lap)
+    observe(4, n1, last)
+    collected(4, 4)
+    tall = tall + raised(n1)
     half = tall.shape[0] // 2
     hi, lo = two(jnp.concatenate([tall[:half], tall[half:]], axis=1))
     narrow = dot(hi, up_xt[...]) + dot(lo, up_xt[...])
@@ -783,13 +796,16 @@
         @pl.when(rim_sends[side])
         def _():
             departed(b1.at[pl.ds(0, 3 * BLOCK)], rim_s.at[side, 0])
-            departed(b3.at[pl.ds(0, 2 * BLOCK)], rim_s.at[side, 1])
+            departed(b3.at[pl.ds(0, BLOCK)], rim_s.at[side, 1])
+            departed(b1.at[pl.ds(0, 2 * BLOCK)], rim_s.at[side, 2])
 
     departed(vels.at[pl.ds(0, SHOTS - 1)], vel_s.at[0])
 
-    @pl.when(lends_low | lends_high)
-    def _():
-        departed(vels.at[pl.ds(0, SHOTS)], vel_s.at[1])
+    for lends, sem in ((lends_low, 1), (lends_high, 2)):
+
+        @pl.when(lends)
+        def _():
+            departed(vels.at[pl.ds(0, SHOTS)], vel_s.at[sem])
 
     departed(recs.at[pl.ds(1, n - 1)], rec_s.at[0])
     departed(grs.at[pl.ds(1, SHOTS - 1)], gr_s.at[0])
@@ -859,12 +875,13 @@
             pltpu.VMEM(fold.shape, BF16),
             pltpu.VMEM((3, CH, (COLS + 2) * 128), BF16),
             pltpu.VMEM((3, CH, (COLS + 2) * 128), BF16),
-            pltpu.VMEM((3 * CH, 9 * CH), BF16),
-            pltpu.VMEM((3 * CH, 9 * CH), BF16),
+            pltpu.VMEM((9 * CH, 3 * CH), BF16),
+            pltpu.VMEM((9 * CH, 3 * CH), BF16),
+            pltpu.VMEM((COLS, 9, CH, 128), F32),
             pltpu.VMEM((COLS * 8, 128), F32),
             pltpu.VMEM((16, FX), BF16),
-            pltpu.VMEM((2 * GROUP, 16, FX), BF16),
-            *[pltpu.VMEM((WINDOW, FX), F32)] * 5,
+            pltpu.VMEM((3 * GROUP, 16, FX), BF16),
+            *[pltpu.VMEM((WINDOW, FX), F32)] * 7,
             *[pltpu.VMEM((WINDOW, FX), BF16)] * 2,
             pltpu.VMEM((STEPS, FPS * FY, FX), BF16),
             pltpu.VMEM(up_y.shape, BF16),
@@ -872,8 +889,8 @@
             pltpu.VMEM((FPS * FY, FX), F32),
             pltpu.VMEM((FPS * FY, FX), F32),
             pltpu.VMEM((WINDOW, FX), F32),
-            pltpu.VMEM((2, BLOCK, FX), BF16),
-            pltpu.VMEM((2, BLOCK, FX), BF16),
+            pltpu.VMEM((2, 2, BLOCK, FX), BF16),
+            pltpu.VMEM((2, 2, BLOCK, FX), BF16),
             pltpu.VMEM((4, 128, BLOCK), BF16),
             pltpu.VMEM((STEPS, 128, FX), F32),
             pltpu.VMEM((STEPS, FX), F32),
@@ -886,9 +903,9 @@
             dma((2, 4)),
             dma((2,)),
             dma((2, 4)),
-            dma((2, 2)),
             dma((2, 3)),
-            dma((2,)),
+            dma((2, 4)),
+            dma((3,)),
             dma((3,)),
             dma((1,)),
             dma((1,)),

time: 40.7 us -> 39 us (0.958)
  Pallas kernels: 39.9 us -> 38.2 us
    pallas_call x1, Pallas kernels: 39 us -> 37.4 us  [body(): pl.pallas_call(functools.partial(kernel, n), out_shape=(pltpu.VMEM((FPS *...]
where the time goes in v3:
time: 39 us; the launch traced here: 38.9 us
  Pallas kernels  38.2 us (98%)
  between operations  0.64 us (2%)
    pallas_call x1, Pallas kernels, body(): pl.pallas_call(functools.partial(kernel, n), out_shape=(pltpu.VMEM((FPS *...  37.4 us
    pallas_call x1, Pallas kernels, body(): pl.pallas_call(hand_over, out_shape=(jax.ShapeDtypeStruct((FPS * FY, FX),...  0.83 us

profile of v3, /device:TPU:0, one launch (start us, length us, event | category | flops | bytes accessed | tf_op | source)
XLA Modules:
  0.0 38.9 jit_solution(18002138058758732847)
XLA Ops:
  0.6 37.4 %shard_map.184 = (f32[1024,128]{1,0:T(8,128)S(1)}, f32[8,4,128]{2,1,0:T(4,128)S(1)}, f32[16,128]{1,0:T(8,128)S(1)}) custom-call(bf16[64,2048]{1,0:T(8,128)(2,1)} %bitcast.13, bf16[27,64,64]{2,1,0:T(8,128)(2,1)} %w1_hbm.1, bf16[27,64,64]{2,1,0:T(8,128)(2,1)} %w2_hbm.1, bf16[1,64]{1,0:T(2,128)(2,1)} %bitcast.17, f32[4,8]{1,0:T(4,128)} %bitcast.15, ...), custom_call_target="tpu_custom_call" | custom-call | tf_op jit(solution)/shard_map/pallas_call | solution.py:852
  38.0 0.8 %shard_map.185 = (f32[1024,128]{1,0:T(8,128)}, f32[8,4,128]{2,1,0:T(4,128)}, f32[16,128]{1,0:T(8,128)}) custom-call(f32[1024,128]{1,0:T(8,128)S(1)} %get-tuple-element.9.a, f32[8,4,128]{2,1,0:T(4,128)S(1)} %get-tuple-element.10.b, f32[16,128]{1,0:T(8,128)S(1)} %get-tuple-element.11.c), custom_call_target="tpu_custom_call" | custom-call | tf_op jit(solution)/shard_map/pallas_call | solution.py:937

commit v4 on v3

--- a/solution.py
+++ b/solution.py
@@ -548,9 +548,6 @@
     lends_high = (shot >= SHOTS - REACH) & has_high
 
     def vel_sends():
-        for j in range(1, SHOTS):
-            vel_copy(lax.rem(shot + j, SHOTS), slab, shot + REACH, 0, 0).start()
-
         @pl.when(lends_low)
         def _():
             for k in range(SHOTS):
@@ -560,6 +557,9 @@
         def _():
             for k in range(SHOTS):
                 vel_copy(k, slab + 1, lax.rem(shot + 2, REACH), 2, 1).start()
+
+        for j in range(1, SHOTS):
+            vel_copy(lax.rem(shot + j, SHOTS), slab, shot + REACH, 0, 0).start()
 
     def vel_gets():
         arrived(vels.at[pl.ds(0, SHOTS - 1)], vel_r.at[0])
@@ -597,15 +597,19 @@
         both = dot(up_y[...], jnp.concatenate([hi, lo], axis=1))
         both = both[:, :FX] + both[:, FX:]
         tall += [both[FY * i : FY * (i + 1)] for i in range(GROUP)]
-    for z in range(-8, FPS + 8):
+    def paced(z):
         i = z // 2 + REACH
-        fine = 0.75 * tall[i] + 0.25 * tall[i + 1 if z % 2 else i - 1]
+        fine = 0.75 * doubled[i] + 0.25 * doubled[i + 1 if z % 2 else i - 1]
         at = z * FY + OWN * BLOCK
         if 0 <= z < FPS:
             speed[z * FY : (z + 1) * FY] = fine
         courant = COURANT * fine
         pace[at : at + FY] = courant * courant * (1.0 / SCALE)
 
+    doubled = tall
+    for z in range(FPS):
+        paced(z)
+
     n1, n2 = jnp.where(has_low, 3, 6), jnp.where(has_low, 4, 5)
     g1, g2 = 9 - n1, 9 - n2
     far_too = has_low & has_high
@@ -615,14 +619,26 @@
 
     for b in (3, 4, 5, 6):
         second(b)
-    step(2, (n2, g2), f2, f1, f3)
-    for c in (4, 5):
-        b3[rows(c)] = f3[rows(c)].astype(BF16)
-    for side in range(2):
-
-        @pl.when(rim_sends[side])
-        def _():
-            rim_copy(side, 3).start()
+    step(2, (n2,), f2, f1, f3)
+    b3[rows(n2)] = f3[rows(n2)].astype(BF16)
+
+    @pl.when(has_low)
+    def _():
+        rim_copy(1, 3).start()
+
+    @pl.when(has_high & jnp.logical_not(has_low))
+    def _():
+        rim_copy(0, 3).start()
+
+    step(2, (g2,), f2, f1, f3)
+
+    @pl.when(far_too)
+    def _():
+        b3[rows(5)] = f3[rows(5)].astype(BF16)
+        rim_copy(0, 3).start()
+
+    for z in (*range(-8, 0), *range(FPS, FPS + 8)):
+        paced(z)
 
     def deeper(side):
         ext, far, last = ((2, 1, 0), (7, 8, 9))[side]

time: 39 us -> 39 us (level)
  no operation moved by 1% of the time
where the time goes in v4:
time: 39 us; the launch traced here: 38.9 us
  Pallas kernels  38.2 us (98%)
  between operations  0.64 us (2%)
    pallas_call x1, Pallas kernels, body(): pl.pallas_call(functools.partial(kernel, n), out_shape=(pltpu.VMEM((FPS *...  37.4 us
    pallas_call x1, Pallas kernels, body(): pl.pallas_call(hand_over, out_shape=(jax.ShapeDtypeStruct((FPS * FY, FX),...  0.83 us

profile of v4, /device:TPU:0, one launch (start us, length us, event | category | flops | bytes accessed | tf_op | source)
XLA Modules:
  0.0 38.9 jit_solution(16738762804183635046)
XLA Ops:
  0.6 37.4 %shard_map.184 = (f32[1024,128]{1,0:T(8,128)S(1)}, f32[8,4,128]{2,1,0:T(4,128)S(1)}, f32[16,128]{1,0:T(8,128)S(1)}) custom-call(bf16[64,2048]{1,0:T(8,128)(2,1)} %bitcast.13, bf16[27,64,64]{2,1,0:T(8,128)(2,1)} %w1_hbm.1, bf16[27,64,64]{2,1,0:T(8,128)(2,1)} %w2_hbm.1, bf16[1,64]{1,0:T(2,128)(2,1)} %bitcast.17, f32[4,8]{1,0:T(4,128)} %bitcast.15, ...), custom_call_target="tpu_custom_call" | custom-call | tf_op jit(solution)/shard_map/pallas_call | solution.py:868
  38.0 0.8 %shard_map.185 = (f32[1024,128]{1,0:T(8,128)}, f32[8,4,128]{2,1,0:T(4,128)}, f32[16,128]{1,0:T(8,128)}) custom-call(f32[1024,128]{1,0:T(8,128)S(1)} %get-tuple-element.9.a, f32[8,4,128]{2,1,0:T(4,128)S(1)} %get-tuple-element.10.b, f32[16,128]{1,0:T(8,128)S(1)} %get-tuple-element.11.c), custom_call_target="tpu_custom_call" | custom-call | tf_op jit(solution)/shard_map/pallas_call | solution.py:953
